TPU v7x, 256 devices: a whole 4x4x8 slice. The times are simulated.
256 devices in a mesh: gx: 16 (over z_hi, x), gy: 16 (over y, z_lo, core).
Axes of the slice: x: 4, y: 4, z: 8 (z_hi: 4, z_lo: 2; z = z_hi * 2 + z_lo), core: 2. Of those that a mesh axis runs over, the one named last changes fastest.
Arguments:
- site_frac: float32 [3, 32, 32, 128], P(None, 'gx', 'gy'), may hold values from 0 to 1
- dual_weight: float32 [32, 32, 128], P('gx', 'gy'), may hold values from -2.5 to 64
- target_mass: float32 [32, 32, 128], P('gx', 'gy'), may hold values from 0.2 to 0.8
- block_list: int32 [16, 16, 12], P('gx', 'gy'), may hold values from 0 to 35, as said below
- block_count: int32 [16, 16], P('gx', 'gy'), may hold values from 1 to 12, as said below
Outputs:
- new_dual: float32 [32, 32, 128], P('gx', 'gy')
- site_shift: float32 [3, 32, 32, 128], P(None, 'gx', 'gy')
- displacement: float32 [3, 64, 64, 256], P(None, 'gx', 'gy')
Inputs may be any that keep to these rules, and one draw needn't show every extreme that they name: `block_list`: within one tile the 12 entries are distinct. The first block_count entries name halo slots whose blocks hold sites of that tile's neighbourhood. `block_count`: some tile uses all 12 entries.
All inputs are finite; a program needn't handle non-finite values.
Results may differ from a plain program's by a relative error of at most 0.0003.
Values sent between devices are 32-bit elements; how exact they have to be, the bound alone decides.
No kernel may reach another device: no remote copies, remote signals or barrier semaphores. Data moves between devices by JAX's collectives and lax.ppermute only.
A program may use at most 64 MiB of HBM per device.

v0:
```python
import math

import jax
import jax.numpy as jnp
from jax import lax
from jax.sharding import PartitionSpec as P

TX = 4
TY = 4
Z = 256


entropy_scale = 0.5
step_rate = 0.5


def with_halo(block, sides, width):
    for axis, dim in sides:
        count = lax.axis_size(axis)
        forward = [(i, i + 1) for i in range(count - 1)]
        forward.append((count - 1, 0))
        backward = [(target, source) for source, target in forward]
        low = lax.ppermute(
            lax.slice_in_dim(block, block.shape[dim] - width, None, axis=dim), axis, forward
        )
        high = lax.ppermute(lax.slice_in_dim(block, 0, width, axis=dim), axis, backward)
        block = jnp.concatenate([low, block, high], axis=dim)
    return block


def from_behind(shard, axis, by):
    peers = lax.axis_size(axis)
    return lax.ppermute(shard, axis, [(i, (i + by) % peers) for i in range(peers)])


def grid_points(first_row, how_many):
    serial = first_row + jnp.arange(how_many)
    cell_x = serial // (TY * Z)
    cell_y = serial // Z % TY
    cell_z = serial % Z
    return jnp.stack([cell_x, cell_y, cell_z]).astype(jnp.float32) + 0.5


def assign(points, chosen, usable, moments):
    spread = points[:, :, None] - chosen[:3, None, :]
    distance = spread[0] * spread[0] + spread[1] * spread[1] + spread[2] * spread[2]
    scores = jnp.where(usable[None, :], (chosen[3][None, :] - distance) / entropy_scale, -jnp.inf)
    peak_score = jnp.max(scores, axis=1, keepdims=True)
    weights = jnp.exp(scores - peak_score)
    shares = weights / jnp.sum(weights, axis=1, keepdims=True)
    masses = jnp.sum(shares, axis=0)
    if not moments:
        return (masses, None, None)
    moment = jnp.sum(shares[None] * spread, axis=1)
    offsets = -jnp.sum(shares[None] * spread, axis=2)
    return (masses, moment, offsets)


def sweep_rows(chosen, usable, moments):
    total_rows = TX * TY * Z
    block_rows = math.gcd(total_rows, 512)
    columns = chosen.shape[1]

    def visit_rows(totals, first_row):
        masses, moment, offsets = assign(
            grid_points(first_row, block_rows), chosen, usable, moments
        )
        if moments:
            return ((totals[0] + masses, totals[1] + moment), offsets)
        return ((totals[0] + masses, totals[1]), offsets)

    start_totals = (jnp.zeros((columns,), jnp.float32), jnp.zeros((3, columns), jnp.float32))
    (masses, moment), gathered = lax.scan(
        visit_rows, start_totals, jnp.arange(0, total_rows, block_rows)
    )
    if not moments:
        return (masses, moment, None)
    return (masses, moment, gathered.transpose(1, 0, 2).reshape(3, total_rows))


def site_stack(site_frac, duals):
    scaling = jnp.array([TX, TY, Z], jnp.float32)
    coords = site_frac * scaling[:, None, None, None]
    return jnp.concatenate([coords, duals[None]], 0)


def place_sites(stacked, per_side):
    offset = (jnp.arange(3 * per_side) // per_side - 1).astype(jnp.float32)
    return jnp.stack(
        [
            stacked[0] + offset[:, None, None] * TX,
            stacked[1] + offset[None, :, None] * TY,
            stacked[2],
            stacked[3],
        ]
    )


def neighbours(stacked, per_side):
    return with_halo(stacked, (("gx", 1), ("gy", 2)), per_side)


def fold_x(spread, per_side):
    lower_rim = spread[:, :per_side]
    middle = spread[:, per_side : 2 * per_side]
    upper_rim = spread[:, 2 * per_side :]
    from_above = from_behind(lower_rim, "gx", -1)
    from_below = from_behind(upper_rim, "gx", 1)
    return middle + from_above + from_below


def fold_y(spread, per_side):
    lower_rim = spread[:, :, :per_side]
    middle = spread[:, :, per_side : 2 * per_side]
    upper_rim = spread[:, :, 2 * per_side :]
    from_above = from_behind(lower_rim, "gy", -1)
    from_below = from_behind(upper_rim, "gy", 1)
    return middle + from_above + from_below


def on_device(site_frac, dual_weight, target_mass, block_list, block_count):
    per_side = site_frac.shape[1]
    block_size = site_frac.shape[3]
    chosen_ids = block_list[0, 0]
    slot_count = chosen_ids.shape[0]
    live_count = block_count[0, 0]
    usable = jnp.arange(slot_count * block_size) // block_size < live_count
    used_blocks = jnp.arange(slot_count) < live_count
    table_size = 9 * per_side * per_side
    placer = (
        (chosen_ids[:, None] == jnp.arange(table_size)[None, :]) & used_blocks[:, None]
    ).astype(jnp.float32)

    def one_step(surround, moments):
        flat_table = surround.reshape(4, table_size, block_size)
        chosen = flat_table[:, chosen_ids].reshape(4, slot_count * block_size)
        masses, moment, offsets = sweep_rows(chosen, usable, moments)
        if moments:
            partials = jnp.concatenate([masses[None], moment], 0)
        else:
            partials = masses[None]
        partials = partials.reshape(-1, slot_count, block_size)
        spread = jnp.einsum("ckb,kt->ctb", partials, placer, precision=lax.Precision.HIGHEST)
        spread = spread.reshape(-1, 3 * per_side, 3 * per_side, block_size)
        folded = fold_y(fold_x(spread, per_side), per_side)
        return (folded, offsets)

    surround = place_sites(neighbours(site_stack(site_frac, dual_weight), per_side), per_side)
    folded, ignored = one_step(surround, False)
    dual_mid = dual_weight + step_rate * (target_mass - folded[0])
    new_duals = with_halo(dual_mid[None], (("gx", 1), ("gy", 2)), per_side)
    surround = jnp.concatenate([surround[:3], new_duals], 0)
    folded, offsets = one_step(surround, True)
    new_dual = dual_mid + step_rate * (target_mass - folded[0])
    site_shift = folded[1:] / (folded[0] + target_mass)[None]
    displacement = offsets.reshape(3, TX, TY, Z)
    return (new_dual, site_shift, displacement)


def solution(mesh):
    in_specs = (
        P(None, "gx", "gy", None),
        P("gx", "gy", None),
        P("gx", "gy", None),
        P("gx", "gy", None),
        P("gx", "gy"),
    )
    out_specs = (P("gx", "gy", None), P(None, "gx", "gy", None), P(None, "gx", "gy", None))
    return jax.shard_map(
        on_device, mesh=mesh, in_specs=in_specs, out_specs=out_specs, check_vma=False
    )
```

profile of v0, /device:TPU:1, one launch (start us, length us, event | category | flops | bytes accessed | tf_op | source)
XLA Modules:
  0.0 197.2 jit_solution(7247664689437033551)
XLA Ops:
  2.1 2.0 %collective-permute-start = (f32[4,2,2,128]{3,2,1,0:T(2,128)S(1)}, f32[4,2,2,128]{3,2,1,0:T(2,128)S(1)}, u32[]{:S(2)}, u32[]{:S(2)}) collective-permute-start(f32[4,2,2,128]{3,2,1,0:T(2,128)S(1)} %pad_maximum_fusion.8), channel_id=1, source_target_pairs={{0,16},{16,32},{32,48},{48,64},{64,80},{80,96},{96,112},{112,128},... | collective-permute-start | bytes 24584 | tf_op jit(solution)/shard_map/ppermute | solution.py:23
  4.1 7.1 %collective-permute-start.1 = (f32[4,2,2,128]{3,2,1,0:T(2,128)S(1)}, f32[4,2,2,128]{3,2,1,0:T(2,128)S(1)}, u32[]{:S(2)}, u32[]{:S(2)}) collective-permute-start(f32[4,2,2,128]{3,2,1,0:T(2,128)S(1)} %pad_maximum_fusion.8), channel_id=1, source_target_pairs={{16,0},{32,16},{48,32},{64,48},{80,64},{96,80},{112,96},{128,112},... | collective-permute-start | bytes 24584 | tf_op jit(solution)/shard_map/ppermute | solution.py:26
  13.3 1.9 collective-permute-start.2
  16.1 2.6 %collective-permute-done.3 = f32[4,6,2,128]{3,2,1,0:T(2,128)S(1)} collective-permute-done((f32[4,6,2,128]{3,2,1,0:T(2,128)S(1)}, f32[4,6,2,128]{3,2,1,0:T(2,128)S(1)}, u32[]{:S(2)}, u32[]{:S(2)}) %collective-permute-start.3) | collective-permute-done | bytes 24608 | tf_op jit(solution)/shard_map/ppermute | solution.py:26
  20.2 48.1 %while.32 = (s32[]{:T(128)}, f32[1536]{0:T(1024)S(1)}, f32[4,1536]{1,0:T(4,128)S(1)}, s32[8]{0:T(128)S(1)}, s32[]{:T(128)}, /*index=5*/s32[]{:T(128)}, s32[]{:T(128)}) while((s32[]{:T(128)}, f32[1536]{0:T(1024)S(1)}, f32[4,1536]{1,0:T(4,128)S(1)}, s32[8]{0:T(128)S(1)}, s32[]{:T(128)}, /*index=5*/s32[]{:T(128)}, s32[]{:T(128)}) %tuple.94), condition=%wide.region_4.5_spmd.clone, body=%wide.region_0.4_spmd.clone.sunk | while | flops 13413891 | bytes 28410988 | solution.py:73
  23.6 1.3 fusion.79
  29.6 1.3 fusion.79
  35.6 1.3 fusion.79
  41.6 1.3 fusion.79
  47.6 1.3 fusion.79
  53.6 1.3 fusion.79
  59.6 1.3 fusion.79
  68.5 6.1 %collective-permute-start.4 = (f32[1,2,6,128]{3,2,1,0:T(8,128)S(1)}, f32[1,2,6,128]{3,2,1,0:T(8,128)S(1)}, u32[]{:S(2)}, u32[]{:S(2)}) collective-permute-start(f32[1,2,6,128]{3,2,1,0:T(8,128)S(1)} %get-tuple-element.324), channel_id=1, source_target_pairs={{0,240},{16,0},{32,16},{48,32},{64,48},{80,64},{96,80},{112,96},{1... | collective-permute-start | bytes 18440 | tf_op jit(solution)/shard_map/ppermute | solution.py:33
  75.4 5.9 %collective-permute-done.5 = f32[1,2,6,128]{3,2,1,0:T(8,128)S(1)} collective-permute-done((f32[1,2,6,128]{3,2,1,0:T(8,128)S(1)}, f32[1,2,6,128]{3,2,1,0:T(8,128)S(1)}, u32[]{:S(2)}, u32[]{:S(2)}) %collective-permute-start.5) | collective-permute-done | bytes 6176 | tf_op jit(solution)/shard_map/ppermute | solution.py:33
  81.4 2.7 %collective-permute-start.6 = (f32[1,2,2,128]{3,2,1,0:T(2,128)S(1)}, f32[1,2,2,128]{3,2,1,0:T(2,128)S(1)}, u32[]{:S(2)}, u32[]{:S(2)}) collective-permute-start(f32[1,2,2,128]{3,2,1,0:T(2,128)S(1)} %get-tuple-element.328), channel_id=1, source_target_pairs={{0,15},{1,0},{2,1},{3,2},{4,3},{5,4},{6,5},{7,6},{8,7},{9,8},{10,9... | collective-permute-start | bytes 6152 | tf_op jit(solution)/shard_map/ppermute | solution.py:33
  84.9 2.2 %collective-permute-done.7 = f32[1,2,2,128]{3,2,1,0:T(2,128)S(1)} collective-permute-done((f32[1,2,2,128]{3,2,1,0:T(2,128)S(1)}, f32[1,2,2,128]{3,2,1,0:T(2,128)S(1)}, u32[]{:S(2)}, u32[]{:S(2)}) %collective-permute-start.7) | collective-permute-done | bytes 2080 | tf_op jit(solution)/shard_map/ppermute | solution.py:33
  87.3 5.7 %collective-permute-start.9 = (f32[1,2,2,128]{3,2,1,0:T(2,128)S(1)}, f32[1,2,2,128]{3,2,1,0:T(2,128)S(1)}, u32[]{:S(2)}, u32[]{:S(2)}) collective-permute-start(f32[1,2,2,128]{3,2,1,0:T(2,128)S(1)} %bitcast.108), channel_id=1, source_target_pairs={{16,0},{32,16},{48,32},{64,48},{80,64},{96,80},{112,96},{128,112},... | collective-permute-start | bytes 6152 | tf_op jit(solution)/shard_map/ppermute | solution.py:26
  93.9 1.4 collective-permute-start.10
  95.3 4.6 %collective-permute-start.11 = (f32[1,6,2,128]{3,2,1,0:T(2,128)S(1)}, f32[1,6,2,128]{3,2,1,0:T(2,128)S(1)}, u32[]{:S(2)}, u32[]{:S(2)}) collective-permute-start(f32[1,6,2,128]{3,2,1,0:T(2,128)S(1)} %pad_maximum_fusion.9), channel_id=1, source_target_pairs={{1,0},{2,1},{3,2},{4,3},{5,4},{6,5},{7,6},{8,7},{9,8},{10,9},{11,1... | collective-permute-start | bytes 18440 | tf_op jit(solution)/shard_map/ppermute | solution.py:26
  101.3 72.6 %while.33 = (s32[]{:T(128)}, f32[1536]{0:T(1024)S(1)}, f32[3,1536]{1,0:T(4,128)S(1)}, f32[8,3,512]{2,1,0:T(4,128)S(1)}, f32[4,1536]{1,0:T(4,128)S(1)}, /*index=5*/s32[8]{0:T(128)S(1)}, s32[]{:T(128)}, s32[]{:T(128)}, s32[]{:T(128)}) while((s32[]{:T(128)}, f32[1536]{0:T(1024)S(1)}, f32[3,1536]{1,0:T(4,128)S(1)}, ...), condition=%wide.region_11.12_spmd.clone, body=%wide.region_5.11_spmd.clone.sunk | while | flops 31506432 | bytes 37996160 | solution.py:73
  107.6 1.9 multiply_reduce_fusion.3
  116.7 1.9 multiply_reduce_fusion.3
  125.7 1.9 multiply_reduce_fusion.3
  134.8 1.9 multiply_reduce_fusion.3
  143.9 1.9 multiply_reduce_fusion.3
  153.0 1.9 multiply_reduce_fusion.3
  162.0 1.9 multiply_reduce_fusion.3
  171.1 1.9 multiply_reduce_fusion.3
  174.3 5.8 %collective-permute-start.12 = (f32[4,2,6,128]{3,2,1,0:T(8,128)S(1)}, f32[4,2,6,128]{3,2,1,0:T(8,128)S(1)}, u32[]{:S(2)}, u32[]{:S(2)}) collective-permute-start(f32[4,2,6,128]{3,2,1,0:T(8,128)S(1)} %copy.25), channel_id=1, source_target_pairs={{0,240},{16,0},{32,16},{48,32},{64,48},{80,64},{96,80},{112,96},{1... | collective-permute-start | bytes 73736 | tf_op jit(solution)/shard_map/ppermute | solution.py:33
  181.1 6.0 %collective-permute-done.13 = f32[4,2,6,128]{3,2,1,0:T(8,128)S(1)} collective-permute-done((f32[4,2,6,128]{3,2,1,0:T(8,128)S(1)}, f32[4,2,6,128]{3,2,1,0:T(8,128)S(1)}, u32[]{:S(2)}, u32[]{:S(2)}) %collective-permute-start.13) | collective-permute-done | bytes 24608 | tf_op jit(solution)/shard_map/ppermute | solution.py:33
  187.1 5.8 %collective-permute-start.14 = (f32[4,2,2,128]{3,2,1,0:T(2,128)S(1)}, f32[4,2,2,128]{3,2,1,0:T(2,128)S(1)}, u32[]{:S(2)}, u32[]{:S(2)}) collective-permute-start(f32[4,2,2,128]{3,2,1,0:T(2,128)S(1)} %get-tuple-element.322), channel_id=1, source_target_pairs={{0,15},{1,0},{2,1},{3,2},{4,3},{5,4},{6,5},{7,6},{8,7},{9,8},{10,9... | collective-permute-start | bytes 24584 | tf_op jit(solution)/shard_map/ppermute | solution.py:33
  193.8 2.2 %collective-permute-done.15 = f32[4,2,2,128]{3,2,1,0:T(2,128)S(1)} collective-permute-done((f32[4,2,2,128]{3,2,1,0:T(2,128)S(1)}, f32[4,2,2,128]{3,2,1,0:T(2,128)S(1)}, u32[]{:S(2)}, u32[]{:S(2)}) %collective-permute-start.15) | collective-permute-done | bytes 8224 | tf_op jit(solution)/shard_map/ppermute | solution.py:33
  (258 shorter events, 108.7 us)
Async XLA Ops:
  2.1 10.5 %collective-permute-start = (f32[4,2,2,128]{3,2,1,0:T(2,128)S(1)}, f32[4,2,2,128]{3,2,1,0:T(2,128)S(1)}, u32[]{:S(2)}, u32[]{:S(2)}) collective-permute-start(f32[4,2,2,128]{3,2,1,0:T(2,128)S(1)} %pad_maximum_fusion.8), channel_id=1, source_target_pairs={{0,16},{16,32},{32,48},{48,64},{64,80},{80,96},{96,112},{112,128},... | collective-permute-start | bytes 24584 | tf_op jit(solution)/shard_map/ppermute | solution.py:23
  4.1 8.4 %collective-permute-start.1 = (f32[4,2,2,128]{3,2,1,0:T(2,128)S(1)}, f32[4,2,2,128]{3,2,1,0:T(2,128)S(1)}, u32[]{:S(2)}, u32[]{:S(2)}) collective-permute-start(f32[4,2,2,128]{3,2,1,0:T(2,128)S(1)} %pad_maximum_fusion.8), channel_id=1, source_target_pairs={{16,0},{32,16},{48,32},{64,48},{80,64},{96,80},{112,96},{128,112},... | collective-permute-start | bytes 24584 | tf_op jit(solution)/shard_map/ppermute | solution.py:26
  13.3 2.8 %collective-permute-start.2 = (f32[4,6,2,128]{3,2,1,0:T(2,128)S(1)}, f32[4,6,2,128]{3,2,1,0:T(2,128)S(1)}, u32[]{:S(2)}, u32[]{:S(2)}) collective-permute-start(f32[4,6,2,128]{3,2,1,0:T(2,128)S(1)} %pad_maximum_fusion.7), channel_id=1, source_target_pairs={{0,1},{1,2},{2,3},{3,4},{4,5},{5,6},{6,7},{7,8},{8,9},{9,10},{10,1... | collective-permute-start | bytes 73736 | tf_op jit(solution)/shard_map/ppermute | solution.py:23
  15.1 3.5 %collective-permute-start.3 = (f32[4,6,2,128]{3,2,1,0:T(2,128)S(1)}, f32[4,6,2,128]{3,2,1,0:T(2,128)S(1)}, u32[]{:S(2)}, u32[]{:S(2)}) collective-permute-start(f32[4,6,2,128]{3,2,1,0:T(2,128)S(1)} %pad_maximum_fusion.7), channel_id=1, source_target_pairs={{1,0},{2,1},{3,2},{4,3},{5,4},{6,5},{7,6},{8,7},{9,8},{10,9},{11,1... | collective-permute-start | bytes 73736 | tf_op jit(solution)/shard_map/ppermute | solution.py:26
  20.2 48.1 %copy-start.2 = (s32[1,1,12]{2,1,0:T(1,128)S(1)}, s32[1,1,12]{2,1,0:T(1,128)}, u32[]{:S(2)}) copy-start(s32[1,1,12]{2,1,0:T(1,128)} %param.13) | copy-start | bytes 148
  20.2 67.0 %copy-start = (f32[2,2,128]{2,1,0:T(2,128)S(1)}, f32[2,2,128]{2,1,0:T(2,128)}, u32[]{:S(2)}) copy-start(f32[2,2,128]{2,1,0:T(2,128)} %param.11) | copy-start | bytes 6148
  20.2 67.0 %copy-start.1 = (f32[2,2,128]{2,1,0:T(2,128)S(1)}, f32[2,2,128]{2,1,0:T(2,128)}, u32[]{:S(2)}) copy-start(f32[2,2,128]{2,1,0:T(2,128)} %param.12) | copy-start | bytes 6148
  68.5 6.9 %collective-permute-start.4 = (f32[1,2,6,128]{3,2,1,0:T(8,128)S(1)}, f32[1,2,6,128]{3,2,1,0:T(8,128)S(1)}, u32[]{:S(2)}, u32[]{:S(2)}) collective-permute-start(f32[1,2,6,128]{3,2,1,0:T(8,128)S(1)} %get-tuple-element.324), channel_id=1, source_target_pairs={{0,240},{16,0},{32,16},{48,32},{64,48},{80,64},{96,80},{112,96},{1... | collective-permute-start | bytes 18440 | tf_op jit(solution)/shard_map/ppermute | solution.py:33
  74.6 6.7 %collective-permute-start.5 = (f32[1,2,6,128]{3,2,1,0:T(8,128)S(1)}, f32[1,2,6,128]{3,2,1,0:T(8,128)S(1)}, u32[]{:S(2)}, u32[]{:S(2)}) collective-permute-start(f32[1,2,6,128]{3,2,1,0:T(8,128)S(1)} %get-tuple-element.325), channel_id=1, source_target_pairs={{0,16},{16,32},{32,48},{48,64},{64,80},{80,96},{96,112},{112,128},... | collective-permute-start | bytes 18440 | tf_op jit(solution)/shard_map/ppermute | solution.py:33
  81.4 3.5 %collective-permute-start.6 = (f32[1,2,2,128]{3,2,1,0:T(2,128)S(1)}, f32[1,2,2,128]{3,2,1,0:T(2,128)S(1)}, u32[]{:S(2)}, u32[]{:S(2)}) collective-permute-start(f32[1,2,2,128]{3,2,1,0:T(2,128)S(1)} %get-tuple-element.328), channel_id=1, source_target_pairs={{0,15},{1,0},{2,1},{3,2},{4,3},{5,4},{6,5},{7,6},{8,7},{9,8},{10,9... | collective-permute-start | bytes 6152 | tf_op jit(solution)/shard_map/ppermute | solution.py:33
  84.1 3.1 %collective-permute-start.7 = (f32[1,2,2,128]{3,2,1,0:T(2,128)S(1)}, f32[1,2,2,128]{3,2,1,0:T(2,128)S(1)}, u32[]{:S(2)}, u32[]{:S(2)}) collective-permute-start(f32[1,2,2,128]{3,2,1,0:T(2,128)S(1)} %get-tuple-element.329), channel_id=1, source_target_pairs={{0,1},{1,2},{2,3},{3,4},{4,5},{5,6},{6,7},{7,8},{8,9},{9,10},{10,1... | collective-permute-start | bytes 6152 | tf_op jit(solution)/shard_map/ppermute | solution.py:33
  87.2 6.7 %collective-permute-start.8 = (f32[1,2,2,128]{3,2,1,0:T(2,128)S(1)}, f32[1,2,2,128]{3,2,1,0:T(2,128)S(1)}, u32[]{:S(2)}, u32[]{:S(2)}) collective-permute-start(f32[1,2,2,128]{3,2,1,0:T(2,128)S(1)} %bitcast.107), channel_id=1, source_target_pairs={{0,16},{16,32},{32,48},{48,64},{64,80},{80,96},{96,112},{112,128},... | collective-permute-start | bytes 6152 | tf_op jit(solution)/shard_map/ppermute | solution.py:23
  87.3 6.6 %collective-permute-start.9 = (f32[1,2,2,128]{3,2,1,0:T(2,128)S(1)}, f32[1,2,2,128]{3,2,1,0:T(2,128)S(1)}, u32[]{:S(2)}, u32[]{:S(2)}) collective-permute-start(f32[1,2,2,128]{3,2,1,0:T(2,128)S(1)} %bitcast.108), channel_id=1, source_target_pairs={{16,0},{32,16},{48,32},{64,48},{80,64},{96,80},{112,96},{128,112},... | collective-permute-start | bytes 6152 | tf_op jit(solution)/shard_map/ppermute | solution.py:26
  93.9 6.5 %collective-permute-start.10 = (f32[1,6,2,128]{3,2,1,0:T(2,128)S(1)}, f32[1,6,2,128]{3,2,1,0:T(2,128)S(1)}, u32[]{:S(2)}, u32[]{:S(2)}) collective-permute-start(f32[1,6,2,128]{3,2,1,0:T(2,128)S(1)} %pad_maximum_fusion.9), channel_id=1, source_target_pairs={{0,1},{1,2},{2,3},{3,4},{4,5},{5,6},{6,7},{7,8},{8,9},{9,10},{10,1... | collective-permute-start | bytes 18440 | tf_op jit(solution)/shard_map/ppermute | solution.py:23
  95.3 5.4 %collective-permute-start.11 = (f32[1,6,2,128]{3,2,1,0:T(2,128)S(1)}, f32[1,6,2,128]{3,2,1,0:T(2,128)S(1)}, u32[]{:S(2)}, u32[]{:S(2)}) collective-permute-start(f32[1,6,2,128]{3,2,1,0:T(2,128)S(1)} %pad_maximum_fusion.9), channel_id=1, source_target_pairs={{1,0},{2,1},{3,2},{4,3},{5,4},{6,5},{7,6},{8,7},{9,8},{10,9},{11,1... | collective-permute-start | bytes 18440 | tf_op jit(solution)/shard_map/ppermute | solution.py:26
  174.3 6.8 %collective-permute-start.12 = (f32[4,2,6,128]{3,2,1,0:T(8,128)S(1)}, f32[4,2,6,128]{3,2,1,0:T(8,128)S(1)}, u32[]{:S(2)}, u32[]{:S(2)}) collective-permute-start(f32[4,2,6,128]{3,2,1,0:T(8,128)S(1)} %copy.25), channel_id=1, source_target_pairs={{0,240},{16,0},{32,16},{48,32},{64,48},{80,64},{96,80},{112,96},{1... | collective-permute-start | bytes 73736 | tf_op jit(solution)/shard_map/ppermute | solution.py:33
  180.1 7.0 %collective-permute-start.13 = (f32[4,2,6,128]{3,2,1,0:T(8,128)S(1)}, f32[4,2,6,128]{3,2,1,0:T(8,128)S(1)}, u32[]{:S(2)}, u32[]{:S(2)}) collective-permute-start(f32[4,2,6,128]{3,2,1,0:T(8,128)S(1)} %copy.26), channel_id=1, source_target_pairs={{0,16},{16,32},{32,48},{48,64},{64,80},{80,96},{96,112},{112,128},... | collective-permute-start | bytes 73736 | tf_op jit(solution)/shard_map/ppermute | solution.py:33
  187.1 6.6 %collective-permute-start.14 = (f32[4,2,2,128]{3,2,1,0:T(2,128)S(1)}, f32[4,2,2,128]{3,2,1,0:T(2,128)S(1)}, u32[]{:S(2)}, u32[]{:S(2)}) collective-permute-start(f32[4,2,2,128]{3,2,1,0:T(2,128)S(1)} %get-tuple-element.322), channel_id=1, source_target_pairs={{0,15},{1,0},{2,1},{3,2},{4,3},{5,4},{6,5},{7,6},{8,7},{9,8},{10,9... | collective-permute-start | bytes 24584 | tf_op jit(solution)/shard_map/ppermute | solution.py:33
  192.9 3.1 %collective-permute-start.15 = (f32[4,2,2,128]{3,2,1,0:T(2,128)S(1)}, f32[4,2,2,128]{3,2,1,0:T(2,128)S(1)}, u32[]{:S(2)}, u32[]{:S(2)}) collective-permute-start(f32[4,2,2,128]{3,2,1,0:T(2,128)S(1)} %get-tuple-element.323), channel_id=1, source_target_pairs={{0,1},{1,2},{2,3},{3,4},{4,5},{5,6},{6,7},{7,8},{8,9},{9,10},{10,1... | collective-permute-start | bytes 24584 | tf_op jit(solution)/shard_map/ppermute | solution.py:33
where the time goes:
time: 199 us; the launch traced here: 197 us
  other arithmetic  114 us (57%)
  starting transfers between devices  43.1 us (22%)
  waiting for transfers between devices  24.5 us (12%)
  local copies, waits for them, and re-layouts  11.8 us (6%)
    ppermute x8, starting transfers between devices, from_behind(): lax.ppermute(shard, axis, [(i, (i + by) % peers) for i in range(peers)])  20.4 us
    reduce_max x16, other arithmetic, assign(): peak_score = jnp.max(scores, axis=1, keepdims=True)  20.1 us
    ppermute x8, waiting for transfers between devices, from_behind(): lax.ppermute(shard, axis, [(i, (i + by) % peers) for i in range(peers)])  19.1 us
    ppermute x4, starting transfers between devices, with_halo(): lax.ppermute(lax.slice_in_dim(block, 0, width, axis=dim), axis, backward)  17.4 us
    reduce_sum x8, other arithmetic, assign(): offsets = -jnp.sum(shares[None] * spread, axis=2)  14.9 us
    reduce_sum x16, other arithmetic, assign(): masses = jnp.sum(shares, axis=0)  13.5 us
    reduce_sum x16, other arithmetic, assign(): shares = weights / jnp.sum(weights, axis=1, keepdims=True)  11.1 us
    sub x16, other arithmetic, assign(): spread = points[:, :, None] - chosen[:3, None, :]  11.1 us
  transfers between devices with their start and end apart: 16, of which 13 were waited for; matrix products, arithmetic and copies ran while one was open for 1% of the time, Pallas kernels for 0%

commit v1 on v0

v1 whole, which is shorter than its diff:
```python
import functools
import math

import jax
import jax.numpy as jnp
from jax import lax
from jax.experimental import pallas as pl
from jax.experimental.pallas import tpu as pltpu
from jax.sharding import PartitionSpec as P

TX = 4
TY = 4
Z = 256
SIDE = 2
BLOCK = 128
K_MAX = 12
SITES = K_MAX * BLOCK
INNER = SIDE * SIDE
HALF = 8

step_rate = 0.5
KAPPA = 2.0 / math.log(2.0)
SHIFT = 44.0
SCALE = 2.0**-20
NEVER = -1.0e7

FIELDS = 24
ROWS = 16
CHUNK = 64


def halves(values):
    high = values.astype(jnp.bfloat16)
    low = (values - high.astype(jnp.float32)).astype(jnp.bfloat16)
    return high, low


def both(values):
    high, low = halves(values)
    high = high.astype(jnp.float32)
    return jnp.concatenate([high, low.astype(jnp.float32)], 0).astype(jnp.bfloat16)


def along_sites(left, right):
    return lax.dot_general(
        left, right, (((1,), (1,)), ((), ())), preferred_element_type=jnp.float32
    )


def along_points(left, right):
    return jnp.dot(left, right, preferred_element_type=jnp.float32)


def joined(sums):
    return sums[:HALF] + sums[HALF : 2 * HALF]


def pass_kernel(moments, ids_ref, count_ref, table_ref, *refs):
    if moments:
        dual_ref, out_ref, disp_ref, site_ref, c_ref, d_ref = refs
    else:
        out_ref, site_ref, c_ref = refs
    count = count_ref[0]
    places = []
    for m in range(K_MAX):
        slot = ids_ref[m]
        row, col = slot // (3 * SIDE), slot % (3 * SIDE)
        tx, ty = row // SIDE, col // SIDE
        inner = row % SIDE * SIDE + col % SIDE
        places.append((tx, ty, inner))
        base = (ty * 3 + tx) * FIELDS + inner
        off_x = ((tx - 1) * TX).astype(jnp.float32)
        off_y = ((ty - 1) * TY).astype(jnp.float32)
        lanes = pl.ds(m * BLOCK, BLOCK)
        site_ref[0:1, lanes] = table_ref[pl.ds(base, 1), :] * TX + off_x
        site_ref[1:2, lanes] = table_ref[pl.ds(base + INNER, 1), :] * TY + off_y
        site_ref[2:3, lanes] = table_ref[pl.ds(base + 2 * INNER, 1), :] * Z
        if moments:
            weight = dual_ref[pl.ds(tx * ROWS + ty * INNER + inner, 1), :]
        else:
            weight = table_ref[pl.ds(base + 3 * INNER, 1), :]
        site_ref[3:4, lanes] = jnp.where(m < count, weight, NEVER)
    site_x, site_y, site_z = site_ref[0:1, :], site_ref[1:2, :], site_ref[2:3, :]
    rel_y = site_y - 2.0
    fixed = site_ref[3:4, :] - rel_y * rel_y
    for g in range(2):
        rel_x = site_x - (1.0 + 2.0 * g)
        site_ref[4 + g : 5 + g, :] = KAPPA * (fixed - rel_x * rel_x)

    def visit(chunk, carry):
        first = pl.multiple_of(chunk * CHUNK, CHUNK)
        rows = pl.ds(first, CHUNK)
        at_z = lax.broadcasted_iota(jnp.int32, (CHUNK, BLOCK), 0) + first
        at_z = at_z.astype(jnp.float32) + 0.5
        peaks = [None, None]
        for m in range(K_MAX):
            lanes = pl.ds(m * BLOCK, BLOCK)
            dz = at_z - site_ref[2:3, lanes]
            fall = dz * dz * -KAPPA
            for g in range(2):
                t = fall + site_ref[4 + g : 5 + g, lanes]
                peaks[g] = t if peaks[g] is None else jnp.maximum(peaks[g], t)
        tops = [jnp.max(p, axis=1, keepdims=True) - SHIFT for p in peaks]
        for m in range(K_MAX):
            lanes = pl.ds(m * BLOCK, BLOCK)
            dz = at_z - site_ref[2:3, lanes]
            fall = dz * dz * -KAPPA
            for g in range(2):
                t = fall + site_ref[4 + g : 5 + g, lanes]
                e = jnp.exp2(t - tops[g])
                c_ref[2 * g, rows, lanes], c_ref[2 * g + 1, rows, lanes] = halves(e)
                if moments:
                    d_ref[2 * g, rows, lanes], d_ref[2 * g + 1, rows, lanes] = halves(e * dz)
        return carry

    lax.fori_loop(0, Z // CHUNK, visit, 0)

    point = lax.broadcasted_iota(jnp.int32, (HALF, SITES), 0)
    at_y = (point % TY).astype(jnp.float32) + 0.5
    sums = [jnp.zeros((1, SITES), jnp.float32) for _ in range(4 if moments else 1)]
    for g in range(2):
        at_x = (point // TY).astype(jnp.float32) + (2.0 * g + 0.5)
        cross = (at_x - (1.0 + 2.0 * g)) * (site_x - (1.0 + 2.0 * g)) + (at_y - 2.0) * rel_y
        a = jnp.exp2((2.0 * KAPPA) * cross - SHIFT)
        c_high, c_low = c_ref[2 * g], c_ref[2 * g + 1]
        if moments:
            ax, ay = a * (at_x - site_x), a * (at_y - site_y)
            d_high, d_low = d_ref[2 * g], d_ref[2 * g + 1]
            a_pair = both(a)
            left = jnp.concatenate([a_pair, both(ax), both(ay)], 0)
            found = along_sites(left, c_high) + along_sites(left, c_low)
            share = 1.0 / joined(found)
            deep = along_sites(a_pair, d_high) + along_sites(a_pair, d_low)
            shown = (joined(found[2 * HALF :]), joined(found[4 * HALF :]), joined(deep))
            for c in range(3):
                value = -(shown[c] * share)
                disp_ref[c, 2 * g] = value[:TY]
                disp_ref[c, 2 * g + 1] = value[TY:]
        else:
            a_pair = both(a)
            share = 1.0 / joined(along_sites(a_pair, c_high) + along_sites(a_pair, c_low))
        pair = both(share * SCALE)
        back = joined(along_points(pair, c_high) + along_points(pair, c_low))
        weighted = [a * back]
        if moments:
            deep = joined(along_points(pair, d_high) + along_points(pair, d_low))
            weighted += [ax * back, ay * back, a * deep]
        for i, part in enumerate(weighted):
            sums[i] = sums[i] + jnp.sum(part, axis=0, keepdims=True)

    out_ref[...] = jnp.zeros_like(out_ref)
    for i, total in enumerate(sums):
        site_ref[i : i + 1, :] = total * (1.0 / SCALE)
    for m in range(K_MAX):
        tx, ty, inner = places[m]
        lanes = pl.ds(m * BLOCK, BLOCK)
        for i in range(len(sums)):
            if moments:
                to = (tx * 3 + ty) * (4 * INNER) + i * INNER + inner
            else:
                to = tx * ROWS + ty * INNER + inner
            out_ref[pl.ds(to, 1), :] = site_ref[i : i + 1, lanes]


def run_pass(ids, count, table, duals=None):
    moments = duals is not None
    smem = pl.BlockSpec(memory_space=pltpu.SMEM)
    vmem = pl.BlockSpec(memory_space=pltpu.VMEM)
    scratch = [
        pltpu.VMEM((8, SITES), jnp.float32),
        pltpu.VMEM((4, Z, SITES), jnp.bfloat16),
    ]
    if moments:
        shapes = (
            jax.ShapeDtypeStruct((9 * 4 * INNER, BLOCK), jnp.float32),
            jax.ShapeDtypeStruct((3, TX, TY, Z), jnp.float32),
        )
        specs, given = (vmem, vmem), (ids, count, table, duals)
        scratch.append(pltpu.VMEM((4, Z, SITES), jnp.bfloat16))
    else:
        shapes = jax.ShapeDtypeStruct((3 * ROWS, BLOCK), jnp.float32)
        specs, given = vmem, (ids, count, table)
    return pl.pallas_call(
        functools.partial(pass_kernel, moments),
        out_shape=shapes,
        in_specs=[smem, smem] + [vmem] * (len(given) - 2),
        out_specs=specs,
        scratch_shapes=scratch,
        compiler_params=pltpu.CompilerParams(vmem_limit_bytes=24 * 2**20),
    )(*given)


def moved(array, axis, by):
    peers = lax.axis_size(axis)
    return lax.ppermute(array, axis, [(i, (i + by) % peers) for i in range(peers)])


def with_sides(array, axis):
    return jnp.concatenate([moved(array, axis, 1), array, moved(array, axis, -1)], 0)


def folded(array, axis):
    third = array.shape[0] // 3
    below, own, above = array[:third], array[third : 2 * third], array[2 * third :]
    return own + moved(above, axis, 1) + moved(below, axis, -1)


def on_device(site_frac, dual_weight, target_mass, block_list, block_count):
    ids = block_list.reshape(K_MAX)
    count = block_count.reshape(1)
    weight = dual_weight.reshape(INNER, BLOCK)
    target = target_mass.reshape(INNER, BLOCK)
    tile = jnp.concatenate(
        [
            site_frac.reshape(3 * INNER, BLOCK),
            weight,
            target,
            jnp.zeros((FIELDS - 5 * INNER, BLOCK), jnp.float32),
        ],
        0,
    )
    table = with_sides(with_sides(tile, "gx"), "gy")

    mass = folded(run_pass(ids, count, table), "gx")
    below, own, above = (mass[i * INNER : (i + 1) * INNER] for i in range(3))
    lower = moved(mass[INNER : 3 * INNER], "gy", 1)
    upper = moved(mass[: 2 * INNER], "gy", -1)
    lowest = moved(above, "gy", 2)
    highest = moved(below, "gy", -2)
    totals = (
        lower[:INNER] + lowest + below,
        own + lower[INNER:] + upper[:INNER],
        upper[INNER:] + above + highest,
    )
    mids = []
    for ty in range(3):
        start = (ty * 3 + 1) * FIELDS
        old = table[start + 3 * INNER : start + 4 * INNER]
        goal = table[start + 4 * INNER : start + 5 * INNER]
        mids.append(old + step_rate * (goal - totals[ty]))
    column = jnp.concatenate([*mids, jnp.zeros((ROWS - 3 * INNER, BLOCK), jnp.float32)], 0)
    duals = with_sides(column, "gx")

    spread, displacement = run_pass(ids, count, table, duals)
    sums = folded(folded(spread, "gx"), "gy")
    mass = sums[:INNER]
    new_dual = mids[1] + step_rate * (target - mass)
    site_shift = sums[INNER:].reshape(3, INNER, BLOCK) / (mass + target)[None]
    return (
        new_dual.reshape(SIDE, SIDE, BLOCK),
        site_shift.reshape(3, SIDE, SIDE, BLOCK),
        displacement,
    )


def solution(mesh):
    in_specs = (
        P(None, "gx", "gy", None),
        P("gx", "gy", None),
        P("gx", "gy", None),
        P("gx", "gy", None),
        P("gx", "gy"),
    )
    out_specs = (P("gx", "gy", None), P(None, "gx", "gy", None), P(None, "gx", "gy", None))
    return jax.shard_map(
        on_device, mesh=mesh, in_specs=in_specs, out_specs=out_specs, check_vma=False
    )
```

time: 199 us -> 83.9 us (0.42)
  the two profiles are of different devices: /device:TPU:1 before, /device:TPU:57 now
where the time goes in v1:
time: 83.9 us; the launch traced here: 83.7 us
  starting transfers between devices  42.9 us (51%)
  waiting for transfers between devices  25.1 us (30%)
  Pallas kernels  11 us (13%)
  local copies, waits for them, and re-layouts  2.21 us (3%)
  between operations  1.37 us (2%)
  other arithmetic  1.24 us (1%)
    ppermute x16, starting transfers between devices, moved(): lax.ppermute(array, axis, [(i, (i + by) % peers) for i in range(peers)])  42.9 us
    ppermute x16, waiting for transfers between devices, moved(): lax.ppermute(array, axis, [(i, (i + by) % peers) for i in range(peers)])  25.1 us
    pallas_call x2, Pallas kernels, run_pass(): pl.pallas_call(functools.partial(pass_kernel, moments), out_shape=shapes,...  11 us
  transfers between devices with their start and end apart: 16, of which 12 were waited for; matrix products, arithmetic and copies ran while one was open for 0% of the time, Pallas kernels for 0%

profile of v1, /device:TPU:57, one launch (start us, length us, event | category | flops | bytes accessed | tf_op | source)
XLA Modules:
  0.0 83.7 jit_solution(13895050356335767789)
XLA Ops:
  0.6 0.7 reshape.36
  1.3 0.7 copy-done.1
  2.0 0.0 copy-done.2
  2.0 7.4 %collective-permute-start.1 = (f32[24,128]{1,0:T(8,128)S(1)}, f32[24,128]{1,0:T(8,128)S(1)}, u32[]{:S(2)}, u32[]{:S(2)}) collective-permute-start(f32[24,128]{1,0:T(8,128)S(1)} %pad_maximum_fusion), channel_id=1, source_target_pairs={{0,240},{16,0},{32,16},{48,32},{64,48},{80,64},{96,80},{112,96},{1... | collective-permute-start | bytes 36872 | tf_op jit(solution)/shard_map/ppermute | solution.py:195
  9.4 0.8 collective-permute-done.1
  10.3 5.9 %collective-permute-done = f32[24,128]{1,0:T(8,128)S(1)} collective-permute-done((f32[24,128]{1,0:T(8,128)S(1)}, f32[24,128]{1,0:T(8,128)S(1)}, u32[]{:S(2)}, u32[]{:S(2)}) %collective-permute-start) | collective-permute-done | bytes 12320 | tf_op jit(solution)/shard_map/ppermute | solution.py:195
  16.2 2.2 %collective-permute-start.3 = (f32[72,128]{1,0:T(8,128)S(1)}, f32[72,128]{1,0:T(8,128)S(1)}, u32[]{:S(2)}, u32[]{:S(2)}) collective-permute-start(f32[72,128]{1,0:T(8,128)S(1)} %concatenate.19), channel_id=1, source_target_pairs={{0,15},{1,0},{2,1},{3,2},{4,3},{5,4},{6,5},{7,6},{8,7},{9,8},{10,9... | collective-permute-start | bytes 110600 | tf_op jit(solution)/shard_map/ppermute | solution.py:195
  18.4 1.8 %collective-permute-start.2 = (f32[72,128]{1,0:T(8,128)S(1)}, f32[72,128]{1,0:T(8,128)S(1)}, u32[]{:S(2)}, u32[]{:S(2)}) collective-permute-start(f32[72,128]{1,0:T(8,128)S(1)} %concatenate.19), channel_id=1, source_target_pairs={{0,1},{1,2},{2,3},{3,4},{4,5},{5,6},{6,7},{7,8},{8,9},{9,10},{10,1... | collective-permute-start | bytes 110600 | tf_op jit(solution)/shard_map/ppermute | solution.py:195
  20.8 1.0 %collective-permute-done.3 = f32[72,128]{1,0:T(8,128)S(1)} collective-permute-done((f32[72,128]{1,0:T(8,128)S(1)}, f32[72,128]{1,0:T(8,128)S(1)}, u32[]{:S(2)}, u32[]{:S(2)}) %collective-permute-start.3) | collective-permute-done | bytes 36896 | tf_op jit(solution)/shard_map/ppermute | solution.py:195
  21.8 0.7 copy-done
  22.5 5.0 %shard_map.76 = f32[48,128]{1,0:T(8,128)S(1)} custom-call(s32[12]{0:T(128)S(1)} %bitcast.8, s32[1]{0:T(128)} %bitcast.6.count_ref, f32[216,128]{1,0:T(8,128)S(1)} %concatenate.20.table_ref), custom_call_target="tpu_custom_call" | custom-call | tf_op jit(solution)/shard_map/pallas_call | solution.py:183
  27.5 0.1 collective-permute-start.4
  27.6 5.7 %collective-permute-start.5 = (f32[16,128]{1,0:T(8,128)S(1)}, f32[16,128]{1,0:T(8,128)S(1)}, u32[]{:S(2)}, u32[]{:S(2)}) collective-permute-start(f32[16,128]{1,0:T(8,128)S(1)} %get-tuple-element.12), channel_id=1, source_target_pairs={{0,240},{16,0},{32,16},{48,32},{64,48},{80,64},{96,80},{112,96},{1... | collective-permute-start | bytes 24584 | tf_op jit(solution)/shard_map/ppermute | solution.py:195
  33.3 1.0 %collective-permute-done.4 = f32[16,128]{1,0:T(8,128)S(1)} collective-permute-done((f32[16,128]{1,0:T(8,128)S(1)}, f32[16,128]{1,0:T(8,128)S(1)}, u32[]{:S(2)}, u32[]{:S(2)}) %collective-permute-start.4) | collective-permute-done | bytes 8224 | tf_op jit(solution)/shard_map/ppermute | solution.py:195
  34.4 5.1 %collective-permute-start.6 = (f32[8,128]{1,0:T(8,128)S(1)}, f32[8,128]{1,0:T(8,128)S(1)}, u32[]{:S(2)}, u32[]{:S(2)}) collective-permute-start(f32[8,128]{1,0:T(8,128)S(1)} %get-tuple-element.20), channel_id=1, source_target_pairs={{0,1},{1,2},{2,3},{3,4},{4,5},{5,6},{6,7},{7,8},{8,9},{9,10},{10,1... | collective-permute-start | bytes 12296 | tf_op jit(solution)/shard_map/ppermute | solution.py:195
  39.5 0.2 collective-permute-start.8
  39.7 1.3 %collective-permute-start.9 = (f32[4,128]{1,0:T(4,128)S(1)}, f32[4,128]{1,0:T(4,128)S(1)}, u32[]{:S(2)}, u32[]{:S(2)}) collective-permute-start(f32[4,128]{1,0:T(4,128)S(1)} %get-tuple-element.19), channel_id=1, source_target_pairs={{0,14},{1,15},{2,0},{3,1},{4,2},{5,3},{6,4},{7,5},{8,6},{9,7},{10,... | collective-permute-start | bytes 6152 | tf_op jit(solution)/shard_map/ppermute | solution.py:195
  40.9 1.0 %collective-permute-done.8 = f32[4,128]{1,0:T(4,128)S(1)} collective-permute-done((f32[4,128]{1,0:T(4,128)S(1)}, f32[4,128]{1,0:T(4,128)S(1)}, u32[]{:S(2)}, u32[]{:S(2)}) %collective-permute-start.8) | collective-permute-done | bytes 2080 | tf_op jit(solution)/shard_map/ppermute | solution.py:195
  41.9 2.3 %collective-permute-done.9 = f32[4,128]{1,0:T(4,128)S(1)} collective-permute-done((f32[4,128]{1,0:T(4,128)S(1)}, f32[4,128]{1,0:T(4,128)S(1)}, u32[]{:S(2)}, u32[]{:S(2)}) %collective-permute-start.9) | collective-permute-done | bytes 2080 | tf_op jit(solution)/shard_map/ppermute | solution.py:195
  44.2 0.4 collective-permute-done.7
  44.6 6.0 %collective-permute-start.11 = (f32[16,128]{1,0:T(8,128)S(1)}, f32[16,128]{1,0:T(8,128)S(1)}, u32[]{:S(2)}, u32[]{:S(2)}) collective-permute-start(f32[16,128]{1,0:T(8,128)S(1)} %pad_maximum_fusion.1), channel_id=1, source_target_pairs={{0,240},{16,0},{32,16},{48,32},{64,48},{80,64},{96,80},{112,96},{1... | collective-permute-start | bytes 24584 | tf_op jit(solution)/shard_map/ppermute | solution.py:195
  50.7 0.8 collective-permute-done.11
  51.4 5.9 %collective-permute-done.10 = f32[16,128]{1,0:T(8,128)S(1)} collective-permute-done((f32[16,128]{1,0:T(8,128)S(1)}, f32[16,128]{1,0:T(8,128)S(1)}, u32[]{:S(2)}, u32[]{:S(2)}) %collective-permute-start.10) | collective-permute-done | bytes 8224 | tf_op jit(solution)/shard_map/ppermute | solution.py:195
  57.4 5.9 %shard_map.77 = (f32[144,128]{1,0:T(8,128)S(1)}, f32[3,4,4,256]{3,2,1,0:T(4,128)}) custom-call(s32[12]{0:T(128)S(1)} %bitcast.9, s32[1]{0:T(128)} %bitcast.7.count_ref, f32[216,128]{1,0:T(8,128)S(1)} %concatenate.20.table_ref, f32[48,128]{1,0:T(8,128)S(1)} %concatenate.22.refs_0_), custom_call_target="tpu_custom_call" | custom-call | tf_op jit(solution)/shard_map/pallas_call | solution.py:183
  63.3 5.7 %collective-permute-start.13 = (f32[48,128]{1,0:T(8,128)S(1)}, f32[48,128]{1,0:T(8,128)S(1)}, u32[]{:S(2)}, u32[]{:S(2)}) collective-permute-start(f32[48,128]{1,0:T(8,128)S(1)} %get-tuple-element.8), channel_id=1, source_target_pairs={{0,240},{16,0},{32,16},{48,32},{64,48},{80,64},{96,80},{112,96},{1... | collective-permute-start | bytes 73736 | tf_op jit(solution)/shard_map/ppermute | solution.py:195
  69.0 1.2 %collective-permute-done.12 = f32[48,128]{1,0:T(8,128)S(1)} collective-permute-done((f32[48,128]{1,0:T(8,128)S(1)}, f32[48,128]{1,0:T(8,128)S(1)}, u32[]{:S(2)}, u32[]{:S(2)}) %collective-permute-start.12) | collective-permute-done | bytes 24608 | tf_op jit(solution)/shard_map/ppermute | solution.py:195
  70.2 7.1 %collective-permute-start.14 = (f32[16,128]{1,0:T(8,128)S(1)}, f32[16,128]{1,0:T(8,128)S(1)}, u32[]{:S(2)}, u32[]{:S(2)}) collective-permute-start(f32[16,128]{1,0:T(8,128)S(1)} %get-tuple-element.9), channel_id=1, source_target_pairs={{0,1},{1,2},{2,3},{3,4},{4,5},{5,6},{6,7},{7,8},{8,9},{9,10},{10,1... | collective-permute-start | bytes 24584 | tf_op jit(solution)/shard_map/ppermute | solution.py:195
  77.3 0.5 collective-permute-start.15
  77.8 0.6 collective-permute-done.14
  78.4 4.1 %collective-permute-done.15 = f32[16,128]{1,0:T(8,128)S(1)} collective-permute-done((f32[16,128]{1,0:T(8,128)S(1)}, f32[16,128]{1,0:T(8,128)S(1)}, u32[]{:S(2)}, u32[]{:S(2)}) %collective-permute-start.15) | collective-permute-done | bytes 8224 | tf_op jit(solution)/shard_map/ppermute | solution.py:195
  82.5 0.6 slice_add_fusion.3
  83.1 0.6 broadcast_divide_fusion
  (28 shorter events, 0.2 us)
Async XLA Ops:
  1.3 0.7 copy-start.1
  1.3 0.7 copy-start.2
  2.0 8.2 %collective-permute-start.1 = (f32[24,128]{1,0:T(8,128)S(1)}, f32[24,128]{1,0:T(8,128)S(1)}, u32[]{:S(2)}, u32[]{:S(2)}) collective-permute-start(f32[24,128]{1,0:T(8,128)S(1)} %pad_maximum_fusion), channel_id=1, source_target_pairs={{0,240},{16,0},{32,16},{48,32},{64,48},{80,64},{96,80},{112,96},{1... | collective-permute-start | bytes 36872 | tf_op jit(solution)/shard_map/ppermute | solution.py:195
  9.4 6.8 %collective-permute-start = (f32[24,128]{1,0:T(8,128)S(1)}, f32[24,128]{1,0:T(8,128)S(1)}, u32[]{:S(2)}, u32[]{:S(2)}) collective-permute-start(f32[24,128]{1,0:T(8,128)S(1)} %pad_maximum_fusion), channel_id=1, source_target_pairs={{0,16},{16,32},{32,48},{48,64},{64,80},{80,96},{96,112},{112,128},... | collective-permute-start | bytes 36872 | tf_op jit(solution)/shard_map/ppermute | solution.py:195
  16.2 5.5 %collective-permute-start.3 = (f32[72,128]{1,0:T(8,128)S(1)}, f32[72,128]{1,0:T(8,128)S(1)}, u32[]{:S(2)}, u32[]{:S(2)}) collective-permute-start(f32[72,128]{1,0:T(8,128)S(1)} %concatenate.19), channel_id=1, source_target_pairs={{0,15},{1,0},{2,1},{3,2},{4,3},{5,4},{6,5},{7,6},{8,7},{9,8},{10,9... | collective-permute-start | bytes 110600 | tf_op jit(solution)/shard_map/ppermute | solution.py:195
  18.4 3.4 %collective-permute-start.2 = (f32[72,128]{1,0:T(8,128)S(1)}, f32[72,128]{1,0:T(8,128)S(1)}, u32[]{:S(2)}, u32[]{:S(2)}) collective-permute-start(f32[72,128]{1,0:T(8,128)S(1)} %concatenate.19), channel_id=1, source_target_pairs={{0,1},{1,2},{2,3},{3,4},{4,5},{5,6},{6,7},{7,8},{8,9},{9,10},{10,1... | collective-permute-start | bytes 110600 | tf_op jit(solution)/shard_map/ppermute | solution.py:195
  21.8 0.7 copy-start
  27.5 6.8 %collective-permute-start.4 = (f32[16,128]{1,0:T(8,128)S(1)}, f32[16,128]{1,0:T(8,128)S(1)}, u32[]{:S(2)}, u32[]{:S(2)}) collective-permute-start(f32[16,128]{1,0:T(8,128)S(1)} %get-tuple-element.11), channel_id=1, source_target_pairs={{0,16},{16,32},{32,48},{48,64},{64,80},{80,96},{96,112},{112,128},... | collective-permute-start | bytes 24584 | tf_op jit(solution)/shard_map/ppermute | solution.py:195
  27.6 6.7 %collective-permute-start.5 = (f32[16,128]{1,0:T(8,128)S(1)}, f32[16,128]{1,0:T(8,128)S(1)}, u32[]{:S(2)}, u32[]{:S(2)}) collective-permute-start(f32[16,128]{1,0:T(8,128)S(1)} %get-tuple-element.12), channel_id=1, source_target_pairs={{0,240},{16,0},{32,16},{48,32},{64,48},{80,64},{96,80},{112,96},{1... | collective-permute-start | bytes 24584 | tf_op jit(solution)/shard_map/ppermute | solution.py:195
  34.4 9.8 %collective-permute-start.6 = (f32[8,128]{1,0:T(8,128)S(1)}, f32[8,128]{1,0:T(8,128)S(1)}, u32[]{:S(2)}, u32[]{:S(2)}) collective-permute-start(f32[8,128]{1,0:T(8,128)S(1)} %get-tuple-element.20), channel_id=1, source_target_pairs={{0,1},{1,2},{2,3},{3,4},{4,5},{5,6},{6,7},{7,8},{8,9},{9,10},{10,1... | collective-permute-start | bytes 12296 | tf_op jit(solution)/shard_map/ppermute | solution.py:195
  39.4 5.1 %collective-permute-start.7 = (f32[8,128]{1,0:T(8,128)S(1)}, f32[8,128]{1,0:T(8,128)S(1)}, u32[]{:S(2)}, u32[]{:S(2)}) collective-permute-start(f32[8,128]{1,0:T(8,128)S(1)} %get-tuple-element.21), channel_id=1, source_target_pairs={{0,15},{1,0},{2,1},{3,2},{4,3},{5,4},{6,5},{7,6},{8,7},{9,8},{10,9... | collective-permute-start | bytes 12296 | tf_op jit(solution)/shard_map/ppermute | solution.py:195
  39.5 2.4 %collective-permute-start.8 = (f32[4,128]{1,0:T(4,128)S(1)}, f32[4,128]{1,0:T(4,128)S(1)}, u32[]{:S(2)}, u32[]{:S(2)}) collective-permute-start(f32[4,128]{1,0:T(4,128)S(1)} %get-tuple-element.18), channel_id=1, source_target_pairs={{0,2},{1,3},{2,4},{3,5},{4,6},{5,7},{6,8},{7,9},{8,10},{9,11},{10,... | collective-permute-start | bytes 6152 | tf_op jit(solution)/shard_map/ppermute | solution.py:195
  39.7 4.5 %collective-permute-start.9 = (f32[4,128]{1,0:T(4,128)S(1)}, f32[4,128]{1,0:T(4,128)S(1)}, u32[]{:S(2)}, u32[]{:S(2)}) collective-permute-start(f32[4,128]{1,0:T(4,128)S(1)} %get-tuple-element.19), channel_id=1, source_target_pairs={{0,14},{1,15},{2,0},{3,1},{4,2},{5,3},{6,4},{7,5},{8,6},{9,7},{10,... | collective-permute-start | bytes 6152 | tf_op jit(solution)/shard_map/ppermute | solution.py:195
  44.6 6.8 %collective-permute-start.11 = (f32[16,128]{1,0:T(8,128)S(1)}, f32[16,128]{1,0:T(8,128)S(1)}, u32[]{:S(2)}, u32[]{:S(2)}) collective-permute-start(f32[16,128]{1,0:T(8,128)S(1)} %pad_maximum_fusion.1), channel_id=1, source_target_pairs={{0,240},{16,0},{32,16},{48,32},{64,48},{80,64},{96,80},{112,96},{1... | collective-permute-start | bytes 24584 | tf_op jit(solution)/shard_map/ppermute | solution.py:195
  50.7 6.7 %collective-permute-start.10 = (f32[16,128]{1,0:T(8,128)S(1)}, f32[16,128]{1,0:T(8,128)S(1)}, u32[]{:S(2)}, u32[]{:S(2)}) collective-permute-start(f32[16,128]{1,0:T(8,128)S(1)} %pad_maximum_fusion.1), channel_id=1, source_target_pairs={{0,16},{16,32},{32,48},{48,64},{64,80},{80,96},{96,112},{112,128},... | collective-permute-start | bytes 24584 | tf_op jit(solution)/shard_map/ppermute | solution.py:195
  63.3 6.9 %collective-permute-start.12 = (f32[48,128]{1,0:T(8,128)S(1)}, f32[48,128]{1,0:T(8,128)S(1)}, u32[]{:S(2)}, u32[]{:S(2)}) collective-permute-start(f32[48,128]{1,0:T(8,128)S(1)} %get-tuple-element.7), channel_id=1, source_target_pairs={{0,16},{16,32},{32,48},{48,64},{64,80},{80,96},{96,112},{112,128},... | collective-permute-start | bytes 73736 | tf_op jit(solution)/shard_map/ppermute | solution.py:195
  63.3 6.9 %collective-permute-start.13 = (f32[48,128]{1,0:T(8,128)S(1)}, f32[48,128]{1,0:T(8,128)S(1)}, u32[]{:S(2)}, u32[]{:S(2)}) collective-permute-start(f32[48,128]{1,0:T(8,128)S(1)} %get-tuple-element.8), channel_id=1, source_target_pairs={{0,240},{16,0},{32,16},{48,32},{64,48},{80,64},{96,80},{112,96},{1... | collective-permute-start | bytes 73736 | tf_op jit(solution)/shard_map/ppermute | solution.py:195
  70.2 8.1 %collective-permute-start.14 = (f32[16,128]{1,0:T(8,128)S(1)}, f32[16,128]{1,0:T(8,128)S(1)}, u32[]{:S(2)}, u32[]{:S(2)}) collective-permute-start(f32[16,128]{1,0:T(8,128)S(1)} %get-tuple-element.9), channel_id=1, source_target_pairs={{0,1},{1,2},{2,3},{3,4},{4,5},{5,6},{6,7},{7,8},{8,9},{9,10},{10,1... | collective-permute-start | bytes 24584 | tf_op jit(solution)/shard_map/ppermute | solution.py:195
  77.3 5.2 %collective-permute-start.15 = (f32[16,128]{1,0:T(8,128)S(1)}, f32[16,128]{1,0:T(8,128)S(1)}, u32[]{:S(2)}, u32[]{:S(2)}) collective-permute-start(f32[16,128]{1,0:T(8,128)S(1)} %get-tuple-element.10), channel_id=1, source_target_pairs={{0,15},{1,0},{2,1},{3,2},{4,3},{5,4},{6,5},{7,6},{8,7},{9,8},{10,9... | collective-permute-start | bytes 24584 | tf_op jit(solution)/shard_map/ppermute | solution.py:195

commit v2 on v1

--- a/solution.py
+++ b/solution.py
@@ -55,30 +55,32 @@
     return sums[:HALF] + sums[HALF : 2 * HALF]
 
 
-def pass_kernel(moments, ids_ref, count_ref, table_ref, *refs):
+def pass_kernel(moments, ids_ref, table_ref, *refs):
     if moments:
-        dual_ref, out_ref, disp_ref, site_ref, c_ref, d_ref = refs
+        mass_ref, out_ref, disp_ref, site_ref, c_ref, d_ref = refs
     else:
         out_ref, site_ref, c_ref = refs
-    count = count_ref[0]
+    count, way_x, way_y = (ids_ref[K_MAX + i] for i in range(3))
     places = []
     for m in range(K_MAX):
         slot = ids_ref[m]
         row, col = slot // (3 * SIDE), slot % (3 * SIDE)
         tx, ty = row // SIDE, col // SIDE
         inner = row % SIDE * SIDE + col % SIDE
-        places.append((tx, ty, inner))
-        base = (ty * 3 + tx) * FIELDS + inner
+        bx, by = 1 + (tx - 1) * way_x, 1 + (ty - 1) * way_y
+        places.append((bx, by, inner))
+        base = (by * 3 + bx) * FIELDS + inner
         off_x = ((tx - 1) * TX).astype(jnp.float32)
         off_y = ((ty - 1) * TY).astype(jnp.float32)
         lanes = pl.ds(m * BLOCK, BLOCK)
         site_ref[0:1, lanes] = table_ref[pl.ds(base, 1), :] * TX + off_x
         site_ref[1:2, lanes] = table_ref[pl.ds(base + INNER, 1), :] * TY + off_y
         site_ref[2:3, lanes] = table_ref[pl.ds(base + 2 * INNER, 1), :] * Z
+        weight = table_ref[pl.ds(base + 3 * INNER, 1), :]
         if moments:
-            weight = dual_ref[pl.ds(tx * ROWS + ty * INNER + inner, 1), :]
-        else:
-            weight = table_ref[pl.ds(base + 3 * INNER, 1), :]
+            goal = table_ref[pl.ds(base + 4 * INNER, 1), :]
+            mass = mass_ref[pl.ds((by * 3 + bx) * INNER + inner, 1), :]
+            weight = weight + step_rate * (goal - mass)
         site_ref[3:4, lanes] = jnp.where(m < count, weight, NEVER)
     site_x, site_y, site_z = site_ref[0:1, :], site_ref[1:2, :], site_ref[2:3, :]
     rel_y = site_y - 2.0
@@ -152,18 +154,18 @@
     for i, total in enumerate(sums):
         site_ref[i : i + 1, :] = total * (1.0 / SCALE)
     for m in range(K_MAX):
-        tx, ty, inner = places[m]
+        bx, by, inner = places[m]
         lanes = pl.ds(m * BLOCK, BLOCK)
         for i in range(len(sums)):
             if moments:
-                to = (tx * 3 + ty) * (4 * INNER) + i * INNER + inner
+                to = (bx * 3 + by) * (4 * INNER) + i * INNER + inner
             else:
-                to = tx * ROWS + ty * INNER + inner
+                to = bx * ROWS + by * INNER + inner
             out_ref[pl.ds(to, 1), :] = site_ref[i : i + 1, lanes]
 
 
-def run_pass(ids, count, table, duals=None):
-    moments = duals is not None
+def run_pass(ids, table, masses=None):
+    moments = masses is not None
     smem = pl.BlockSpec(memory_space=pltpu.SMEM)
     vmem = pl.BlockSpec(memory_space=pltpu.VMEM)
     scratch = [
@@ -175,39 +177,70 @@
             jax.ShapeDtypeStruct((9 * 4 * INNER, BLOCK), jnp.float32),
             jax.ShapeDtypeStruct((3, TX, TY, Z), jnp.float32),
         )
-        specs, given = (vmem, vmem), (ids, count, table, duals)
+        specs, given = (vmem, vmem), (ids, table, masses)
         scratch.append(pltpu.VMEM((4, Z, SITES), jnp.bfloat16))
     else:
         shapes = jax.ShapeDtypeStruct((3 * ROWS, BLOCK), jnp.float32)
-        specs, given = vmem, (ids, count, table)
+        specs, given = vmem, (ids, table)
     return pl.pallas_call(
         functools.partial(pass_kernel, moments),
         out_shape=shapes,
-        in_specs=[smem, smem] + [vmem] * (len(given) - 2),
+        in_specs=[smem] + [vmem] * (len(given) - 1),
         out_specs=specs,
         scratch_shapes=scratch,
         compiler_params=pltpu.CompilerParams(vmem_limit_bytes=24 * 2**20),
     )(*given)
 
 
-def moved(array, axis, by):
+def partner(kind, i, peers):
+    if kind == "even":
+        return i ^ 1
+    if kind == "odd":
+        return (i + 1 if i % 2 else i - 1) % peers
+    if kind == "even2":
+        return i ^ 2
+    return (i + 2 if i % 4 >= 2 else i - 2) % peers
+
+
+def swapped(array, axis, kind):
     peers = lax.axis_size(axis)
-    return lax.ppermute(array, axis, [(i, (i + by) % peers) for i in range(peers)])
+    return lax.ppermute(array, axis, [(i, partner(kind, i, peers)) for i in range(peers)])
 
 
 def with_sides(array, axis):
-    return jnp.concatenate([moved(array, axis, 1), array, moved(array, axis, -1)], 0)
+    return jnp.concatenate([swapped(array, axis, "even"), array, swapped(array, axis, "odd")], 0)
 
 
 def folded(array, axis):
     third = array.shape[0] // 3
-    below, own, above = array[:third], array[third : 2 * third], array[2 * third :]
-    return own + moved(above, axis, 1) + moved(below, axis, -1)
+    return (
+        array[third : 2 * third]
+        + swapped(array[:third], axis, "even")
+        + swapped(array[2 * third :], axis, "odd")
+    )
+
+
+def folded_with_sides(blocks, axis):
+    even, own, odd = blocks
+    rows = own.shape[0]
+    place = lax.axis_index(axis) % 4
+    outer = (place == 0) | (place == 3)
+    near_even = swapped(jnp.concatenate([own, even], 0), axis, "even")
+    far_even = swapped(jnp.where(outer, even, odd), axis, "even2")
+    near_odd = swapped(jnp.concatenate([own, odd], 0), axis, "odd")
+    far_odd = swapped(jnp.where(outer, odd, even), axis, "odd2")
+    return (
+        near_even[:rows] + even + jnp.where(outer, far_even, far_odd),
+        own + near_even[rows:] + near_odd[rows:],
+        near_odd[:rows] + odd + jnp.where(outer, far_odd, far_even),
+    )
 
 
 def on_device(site_frac, dual_weight, target_mass, block_list, block_count):
-    ids = block_list.reshape(K_MAX)
-    count = block_count.reshape(1)
+    ways = [2 * (lax.axis_index(axis) % 2) - 1 for axis in ("gx", "gy")]
+    ids = jnp.concatenate(
+        [block_list.reshape(K_MAX), block_count.reshape(1), jnp.stack(ways).astype(jnp.int32)]
+    )
     weight = dual_weight.reshape(INNER, BLOCK)
     target = target_mass.reshape(INNER, BLOCK)
     tile = jnp.concatenate(
@@ -221,30 +254,18 @@
     )
     table = with_sides(with_sides(tile, "gx"), "gy")
 
-    mass = folded(run_pass(ids, count, table), "gx")
-    below, own, above = (mass[i * INNER : (i + 1) * INNER] for i in range(3))
-    lower = moved(mass[INNER : 3 * INNER], "gy", 1)
-    upper = moved(mass[: 2 * INNER], "gy", -1)
-    lowest = moved(above, "gy", 2)
-    highest = moved(below, "gy", -2)
-    totals = (
-        lower[:INNER] + lowest + below,
-        own + lower[INNER:] + upper[:INNER],
-        upper[INNER:] + above + highest,
-    )
-    mids = []
-    for ty in range(3):
-        start = (ty * 3 + 1) * FIELDS
-        old = table[start + 3 * INNER : start + 4 * INNER]
-        goal = table[start + 4 * INNER : start + 5 * INNER]
-        mids.append(old + step_rate * (goal - totals[ty]))
-    column = jnp.concatenate([*mids, jnp.zeros((ROWS - 3 * INNER, BLOCK), jnp.float32)], 0)
-    duals = with_sides(column, "gx")
-
-    spread, displacement = run_pass(ids, count, table, duals)
+    partial = run_pass(ids, table)
+    blocks = folded_with_sides([partial[i * ROWS : i * ROWS + 3 * INNER] for i in range(3)], "gx")
+    rims = [
+        jnp.concatenate([b[j * INNER : (j + 1) * INNER] for b in blocks], 0) for j in range(3)
+    ]
+    masses = jnp.concatenate(folded_with_sides(rims, "gy"), 0)
+
+    spread, displacement = run_pass(ids, table, masses)
     sums = folded(folded(spread, "gx"), "gy")
     mass = sums[:INNER]
-    new_dual = mids[1] + step_rate * (target - mass)
+    mid = weight + step_rate * (target - masses[4 * INNER : 5 * INNER])
+    new_dual = mid + step_rate * (target - mass)
     site_shift = sums[INNER:].reshape(3, INNER, BLOCK) / (mass + target)[None]
     return (
         new_dual.reshape(SIDE, SIDE, BLOCK),

time: 83.9 us -> 67.8 us (0.81)
  the two profiles are of different devices: /device:TPU:57 before, /device:TPU:1 now
where the time goes in v2:
time: 67.8 us; the launch traced here: 67.6 us
  starting transfers between devices  35.8 us (53%)
  waiting for transfers between devices  15.8 us (23%)
  Pallas kernels  11 us (16%)
  local copies, waits for them, and re-layouts  2.29 us (3%)
  between operations  1.37 us (2%)
  other arithmetic  1.35 us (2%)
    ppermute x16, starting transfers between devices, swapped(): lax.ppermute(array, axis, [(i, partner(kind, i, peers)) for i in range(pe...  35.8 us
    ppermute x16, waiting for transfers between devices, swapped(): lax.ppermute(array, axis, [(i, partner(kind, i, peers)) for i in range(pe...  15.8 us
    pallas_call x2, Pallas kernels, run_pass(): pl.pallas_call(functools.partial(pass_kernel, moments), out_shape=shapes,...  11 us
  transfers between devices with their start and end apart: 16, of which 10 were waited for; matrix products, arithmetic and copies ran while one was open for 0% of the time, Pallas kernels for 0%

profile of v2, /device:TPU:1, one launch (start us, length us, event | category | flops | bytes accessed | tf_op | source)
XLA Modules:
  0.0 67.6 jit_solution(6548169897187868301)
XLA Ops:
  0.6 0.7 %reshape.36 = f32[12,128]{1,0:T(8,128)S(1)} reshape(f32[3,2,2,128]{3,2,1,0:T(2,128)} %param.5) | data formatting | bytes 12288 | tf_op jit(solution)/shard_map/reshape | solution.py:248
  1.3 0.7 copy-done
  2.0 9.1 %collective-permute-start.1 = (f32[24,128]{1,0:T(8,128)S(1)}, f32[24,128]{1,0:T(8,128)S(1)}, u32[]{:S(2)}, u32[]{:S(2)}) collective-permute-start(f32[24,128]{1,0:T(8,128)S(1)} %pad_maximum_fusion.3), channel_id=1, source_target_pairs={{0,240},{16,32},{32,16},{48,64},{64,48},{80,96},{96,80},{112,128},... | collective-permute-start | bytes 36872 | tf_op jit(solution)/shard_map/ppermute | solution.py:207
  11.8 0.4 collective-permute-done.1
  12.2 1.5 %collective-permute-done = f32[24,128]{1,0:T(8,128)S(1)} collective-permute-done((f32[24,128]{1,0:T(8,128)S(1)}, f32[24,128]{1,0:T(8,128)S(1)}, u32[]{:S(2)}, u32[]{:S(2)}) %collective-permute-start) | collective-permute-done | bytes 12320 | tf_op jit(solution)/shard_map/ppermute | solution.py:207
  13.7 2.8 %collective-permute-start.3 = (f32[72,128]{1,0:T(8,128)S(1)}, f32[72,128]{1,0:T(8,128)S(1)}, u32[]{:S(2)}, u32[]{:S(2)}) collective-permute-start(f32[72,128]{1,0:T(8,128)S(1)} %concatenate.42), channel_id=1, source_target_pairs={{0,15},{1,2},{2,1},{3,4},{4,3},{5,6},{6,5},{7,8},{8,7},{9,10},{10,... | collective-permute-start | bytes 110600 | tf_op jit(solution)/shard_map/ppermute | solution.py:207
  16.5 0.9 %collective-permute-start.2 = (f32[72,128]{1,0:T(8,128)S(1)}, f32[72,128]{1,0:T(8,128)S(1)}, u32[]{:S(2)}, u32[]{:S(2)}) collective-permute-start(f32[72,128]{1,0:T(8,128)S(1)} %concatenate.42), channel_id=1, source_target_pairs={{0,1},{1,0},{2,3},{3,2},{4,5},{5,4},{6,7},{7,6},{8,9},{9,8},{10,11... | collective-permute-start | bytes 110600 | tf_op jit(solution)/shard_map/ppermute | solution.py:207
  17.4 0.7 copy-done.2
  18.1 0.1 pad_add_fusion.ids_ref
  18.1 0.1 collective-permute-done.3
  18.2 0.1 collective-permute-done.2
  18.3 5.1 %shard_map.76 = f32[48,128]{1,0:T(8,128)S(1)} custom-call(s32[15]{0:T(128)S(1)} %pad_add_fusion.ids_ref, f32[216,128]{1,0:T(8,128)S(1)} %concatenate.43.table_ref), custom_call_target="tpu_custom_call" | custom-call | tf_op jit(solution)/shard_map/pallas_call | solution.py:185
  23.4 4.3 %collective-permute-start.7 = (f32[24,128]{1,0:T(8,128)S(1)}, f32[24,128]{1,0:T(8,128)S(1)}, u32[]{:S(2)}, u32[]{:S(2)}) collective-permute-start(f32[24,128]{1,0:T(8,128)S(1)} %get-tuple-element.35), channel_id=1, source_target_pairs={{0,240},{16,32},{32,16},{48,64},{64,48},{80,96},{96,80},{112,128},... | collective-permute-start | bytes 36872 | tf_op jit(solution)/shard_map/ppermute | solution.py:207
  27.7 2.6 %collective-permute-start.6 = (f32[12,128]{1,0:T(8,128)S(1)}, f32[12,128]{1,0:T(8,128)S(1)}, u32[]{:S(2)}, u32[]{:S(2)}) collective-permute-start(f32[12,128]{1,0:T(8,128)S(1)} %get-tuple-element.16), channel_id=1, source_target_pairs={{0,224},{16,240},{32,64},{48,80},{64,32},{80,48},{96,128},{112,144... | collective-permute-start | bytes 18440 | tf_op jit(solution)/shard_map/ppermute | solution.py:207
  30.4 1.4 %collective-permute-done.5 = f32[12,128]{1,0:T(8,128)S(1)} collective-permute-done((f32[12,128]{1,0:T(8,128)S(1)}, f32[12,128]{1,0:T(8,128)S(1)}, u32[]{:S(2)}, u32[]{:S(2)}) %collective-permute-start.5) | collective-permute-done | bytes 6176 | tf_op jit(solution)/shard_map/ppermute | solution.py:207
  31.7 3.0 %collective-permute-done.6 = f32[12,128]{1,0:T(8,128)S(1)} collective-permute-done((f32[12,128]{1,0:T(8,128)S(1)}, f32[12,128]{1,0:T(8,128)S(1)}, u32[]{:S(2)}, u32[]{:S(2)}) %collective-permute-start.6) | collective-permute-done | bytes 6176 | tf_op jit(solution)/shard_map/ppermute | solution.py:207
  34.8 0.1 concatenate.48
  34.8 2.9 %collective-permute-start.9 = (f32[24,128]{1,0:T(8,128)S(1)}, f32[24,128]{1,0:T(8,128)S(1)}, u32[]{:S(2)}, u32[]{:S(2)}) collective-permute-start(f32[24,128]{1,0:T(8,128)S(1)} %concatenate.48), channel_id=1, source_target_pairs={{0,15},{1,2},{2,1},{3,4},{4,3},{5,6},{6,5},{7,8},{8,7},{9,10},{10,... | collective-permute-start | bytes 36872 | tf_op jit(solution)/shard_map/ppermute | solution.py:207
  37.7 0.1 concatenate.47
  37.8 1.9 %collective-permute-start.8 = (f32[24,128]{1,0:T(8,128)S(1)}, f32[24,128]{1,0:T(8,128)S(1)}, u32[]{:S(2)}, u32[]{:S(2)}) collective-permute-start(f32[24,128]{1,0:T(8,128)S(1)} %concatenate.47), channel_id=1, source_target_pairs={{0,1},{1,0},{2,3},{3,2},{4,5},{5,4},{6,7},{7,6},{8,9},{9,8},{10,11... | collective-permute-start | bytes 36872 | tf_op jit(solution)/shard_map/ppermute | solution.py:207
  39.7 0.9 %collective-permute-start.10 = (f32[12,128]{1,0:T(8,128)S(1)}, f32[12,128]{1,0:T(8,128)S(1)}, u32[]{:S(2)}, u32[]{:S(2)}) collective-permute-start(f32[12,128]{1,0:T(8,128)S(1)} %get-tuple-element.22), channel_id=1, source_target_pairs={{0,2},{1,3},{2,0},{3,1},{4,6},{5,7},{6,4},{7,5},{8,10},{9,11},{10,... | collective-permute-start | bytes 18440 | tf_op jit(solution)/shard_map/ppermute | solution.py:207
  40.6 2.7 %collective-permute-start.11 = (f32[12,128]{1,0:T(8,128)S(1)}, f32[12,128]{1,0:T(8,128)S(1)}, u32[]{:S(2)}, u32[]{:S(2)}) collective-permute-start(f32[12,128]{1,0:T(8,128)S(1)} %get-tuple-element.23), channel_id=1, source_target_pairs={{0,14},{1,15},{2,4},{3,5},{4,2},{5,3},{6,8},{7,9},{8,6},{9,7},{10,... | collective-permute-start | bytes 18440 | tf_op jit(solution)/shard_map/ppermute | solution.py:207
  43.3 1.9 %collective-permute-done.11 = f32[12,128]{1,0:T(8,128)S(1)} collective-permute-done((f32[12,128]{1,0:T(8,128)S(1)}, f32[12,128]{1,0:T(8,128)S(1)}, u32[]{:S(2)}, u32[]{:S(2)}) %collective-permute-start.11) | collective-permute-done | bytes 6176 | tf_op jit(solution)/shard_map/ppermute | solution.py:207
  45.3 5.9 %shard_map.77 = (f32[144,128]{1,0:T(8,128)S(1)}, f32[3,4,4,256]{3,2,1,0:T(4,128)}) custom-call(s32[15]{0:T(128)S(1)} %pad_add_fusion.ids_ref, f32[216,128]{1,0:T(8,128)S(1)} %concatenate.43.table_ref, f32[36,128]{1,0:T(8,128)S(1)} %pad_maximum_fusion.refs_0_), custom_call_target="tpu_custom_call" | custom-call | tf_op jit(solution)/shard_map/pallas_call | solution.py:185
  51.2 1.7 %collective-permute-start.12 = (f32[48,128]{1,0:T(8,128)S(1)}, f32[48,128]{1,0:T(8,128)S(1)}, u32[]{:S(2)}, u32[]{:S(2)}) collective-permute-start(f32[48,128]{1,0:T(8,128)S(1)} %get-tuple-element.7), channel_id=1, source_target_pairs={{0,16},{16,0},{32,48},{48,32},{64,80},{80,64},{96,112},{112,96},{1... | collective-permute-start | bytes 73736 | tf_op jit(solution)/shard_map/ppermute | solution.py:207
  52.9 2.4 %collective-permute-start.13 = (f32[48,128]{1,0:T(8,128)S(1)}, f32[48,128]{1,0:T(8,128)S(1)}, u32[]{:S(2)}, u32[]{:S(2)}) collective-permute-start(f32[48,128]{1,0:T(8,128)S(1)} %get-tuple-element.8), channel_id=1, source_target_pairs={{0,240},{16,32},{32,16},{48,64},{64,48},{80,96},{96,80},{112,128},... | collective-permute-start | bytes 73736 | tf_op jit(solution)/shard_map/ppermute | solution.py:207
  55.4 4.4 %collective-permute-done.13 = f32[48,128]{1,0:T(8,128)S(1)} collective-permute-done((f32[48,128]{1,0:T(8,128)S(1)}, f32[48,128]{1,0:T(8,128)S(1)}, u32[]{:S(2)}, u32[]{:S(2)}) %collective-permute-start.13) | collective-permute-done | bytes 24608 | tf_op jit(solution)/shard_map/ppermute | solution.py:207
  59.8 3.4 %collective-permute-start.14 = (f32[16,128]{1,0:T(8,128)S(1)}, f32[16,128]{1,0:T(8,128)S(1)}, u32[]{:S(2)}, u32[]{:S(2)}) collective-permute-start(f32[16,128]{1,0:T(8,128)S(1)} %get-tuple-element.12), channel_id=1, source_target_pairs={{0,1},{1,0},{2,3},{3,2},{4,5},{5,4},{6,7},{7,6},{8,9},{9,8},{10,11... | collective-permute-start | bytes 24584 | tf_op jit(solution)/shard_map/ppermute | solution.py:207
  63.3 0.8 %collective-permute-done.14 = f32[16,128]{1,0:T(8,128)S(1)} collective-permute-done((f32[16,128]{1,0:T(8,128)S(1)}, f32[16,128]{1,0:T(8,128)S(1)}, u32[]{:S(2)}, u32[]{:S(2)}) %collective-permute-start.14) | collective-permute-done | bytes 8224 | tf_op jit(solution)/shard_map/ppermute | solution.py:207
  64.1 2.2 %collective-permute-done.15 = f32[16,128]{1,0:T(8,128)S(1)} collective-permute-done((f32[16,128]{1,0:T(8,128)S(1)}, f32[16,128]{1,0:T(8,128)S(1)}, u32[]{:S(2)}, u32[]{:S(2)}) %collective-permute-start.15) | collective-permute-done | bytes 8224 | tf_op jit(solution)/shard_map/ppermute | solution.py:207
  66.4 0.6 slice_add_fusion.9
  67.0 0.6 broadcast_divide_fusion
  (32 shorter events, 0.3 us)
Async XLA Ops:
  1.3 0.7 %copy-start = (f32[2,2,128]{2,1,0:T(2,128)S(1)}, f32[2,2,128]{2,1,0:T(2,128)}, u32[]{:S(2)}) copy-start(f32[2,2,128]{2,1,0:T(2,128)} %param.7) | copy-start | bytes 6148
  1.3 0.7 %copy-start.1 = (f32[2,2,128]{2,1,0:T(2,128)S(1)}, f32[2,2,128]{2,1,0:T(2,128)}, u32[]{:S(2)}) copy-start(f32[2,2,128]{2,1,0:T(2,128)} %param.6) | copy-start | bytes 6148
  2.0 10.2 %collective-permute-start.1 = (f32[24,128]{1,0:T(8,128)S(1)}, f32[24,128]{1,0:T(8,128)S(1)}, u32[]{:S(2)}, u32[]{:S(2)}) collective-permute-start(f32[24,128]{1,0:T(8,128)S(1)} %pad_maximum_fusion.3), channel_id=1, source_target_pairs={{0,240},{16,32},{32,16},{48,64},{64,48},{80,96},{96,80},{112,128},... | collective-permute-start | bytes 36872 | tf_op jit(solution)/shard_map/ppermute | solution.py:207
  11.2 2.5 %collective-permute-start = (f32[24,128]{1,0:T(8,128)S(1)}, f32[24,128]{1,0:T(8,128)S(1)}, u32[]{:S(2)}, u32[]{:S(2)}) collective-permute-start(f32[24,128]{1,0:T(8,128)S(1)} %pad_maximum_fusion.3), channel_id=1, source_target_pairs={{0,16},{16,0},{32,48},{48,32},{64,80},{80,64},{96,112},{112,96},{1... | collective-permute-start | bytes 36872 | tf_op jit(solution)/shard_map/ppermute | solution.py:207
  13.7 4.4 %collective-permute-start.3 = (f32[72,128]{1,0:T(8,128)S(1)}, f32[72,128]{1,0:T(8,128)S(1)}, u32[]{:S(2)}, u32[]{:S(2)}) collective-permute-start(f32[72,128]{1,0:T(8,128)S(1)} %concatenate.42), channel_id=1, source_target_pairs={{0,15},{1,2},{2,1},{3,4},{4,3},{5,6},{6,5},{7,8},{8,7},{9,10},{10,... | collective-permute-start | bytes 110600 | tf_op jit(solution)/shard_map/ppermute | solution.py:207
  16.5 1.7 %collective-permute-start.2 = (f32[72,128]{1,0:T(8,128)S(1)}, f32[72,128]{1,0:T(8,128)S(1)}, u32[]{:S(2)}, u32[]{:S(2)}) collective-permute-start(f32[72,128]{1,0:T(8,128)S(1)} %concatenate.42), channel_id=1, source_target_pairs={{0,1},{1,0},{2,3},{3,2},{4,5},{5,4},{6,7},{7,6},{8,9},{9,8},{10,11... | collective-permute-start | bytes 110600 | tf_op jit(solution)/shard_map/ppermute | solution.py:207
  17.4 0.7 copy-start.2
  23.4 11.3 %collective-permute-start.7 = (f32[24,128]{1,0:T(8,128)S(1)}, f32[24,128]{1,0:T(8,128)S(1)}, u32[]{:S(2)}, u32[]{:S(2)}) collective-permute-start(f32[24,128]{1,0:T(8,128)S(1)} %get-tuple-element.35), channel_id=1, source_target_pairs={{0,240},{16,32},{32,16},{48,64},{64,48},{80,96},{96,80},{112,128},... | collective-permute-start | bytes 36872 | tf_op jit(solution)/shard_map/ppermute | solution.py:207
  27.7 7.0 %collective-permute-start.4 = (f32[24,128]{1,0:T(8,128)S(1)}, f32[24,128]{1,0:T(8,128)S(1)}, u32[]{:S(2)}, u32[]{:S(2)}) collective-permute-start(f32[24,128]{1,0:T(8,128)S(1)} %get-tuple-element.36), channel_id=1, source_target_pairs={{0,16},{16,0},{32,48},{48,32},{64,80},{80,64},{96,112},{112,96},{1... | collective-permute-start | bytes 36872 | tf_op jit(solution)/shard_map/ppermute | solution.py:207
  27.7 4.0 %collective-permute-start.5 = (f32[12,128]{1,0:T(8,128)S(1)}, f32[12,128]{1,0:T(8,128)S(1)}, u32[]{:S(2)}, u32[]{:S(2)}) collective-permute-start(f32[12,128]{1,0:T(8,128)S(1)} %get-tuple-element.15), channel_id=1, source_target_pairs={{0,32},{16,48},{32,0},{48,16},{64,96},{80,112},{96,64},{112,80},{1... | collective-permute-start | bytes 18440 | tf_op jit(solution)/shard_map/ppermute | solution.py:207
  27.7 7.0 %collective-permute-start.6 = (f32[12,128]{1,0:T(8,128)S(1)}, f32[12,128]{1,0:T(8,128)S(1)}, u32[]{:S(2)}, u32[]{:S(2)}) collective-permute-start(f32[12,128]{1,0:T(8,128)S(1)} %get-tuple-element.16), channel_id=1, source_target_pairs={{0,224},{16,240},{32,64},{48,80},{64,32},{80,48},{96,128},{112,144... | collective-permute-start | bytes 18440 | tf_op jit(solution)/shard_map/ppermute | solution.py:207
  34.8 10.4 %collective-permute-start.9 = (f32[24,128]{1,0:T(8,128)S(1)}, f32[24,128]{1,0:T(8,128)S(1)}, u32[]{:S(2)}, u32[]{:S(2)}) collective-permute-start(f32[24,128]{1,0:T(8,128)S(1)} %concatenate.48), channel_id=1, source_target_pairs={{0,15},{1,2},{2,1},{3,4},{4,3},{5,6},{6,5},{7,8},{8,7},{9,10},{10,... | collective-permute-start | bytes 36872 | tf_op jit(solution)/shard_map/ppermute | solution.py:207
  37.8 7.4 %collective-permute-start.8 = (f32[24,128]{1,0:T(8,128)S(1)}, f32[24,128]{1,0:T(8,128)S(1)}, u32[]{:S(2)}, u32[]{:S(2)}) collective-permute-start(f32[24,128]{1,0:T(8,128)S(1)} %concatenate.47), channel_id=1, source_target_pairs={{0,1},{1,0},{2,3},{3,2},{4,5},{5,4},{6,7},{7,6},{8,9},{9,8},{10,11... | collective-permute-start | bytes 36872 | tf_op jit(solution)/shard_map/ppermute | solution.py:207
  39.7 3.7 %collective-permute-start.10 = (f32[12,128]{1,0:T(8,128)S(1)}, f32[12,128]{1,0:T(8,128)S(1)}, u32[]{:S(2)}, u32[]{:S(2)}) collective-permute-start(f32[12,128]{1,0:T(8,128)S(1)} %get-tuple-element.22), channel_id=1, source_target_pairs={{0,2},{1,3},{2,0},{3,1},{4,6},{5,7},{6,4},{7,5},{8,10},{9,11},{10,... | collective-permute-start | bytes 18440 | tf_op jit(solution)/shard_map/ppermute | solution.py:207
  40.6 4.6 %collective-permute-start.11 = (f32[12,128]{1,0:T(8,128)S(1)}, f32[12,128]{1,0:T(8,128)S(1)}, u32[]{:S(2)}, u32[]{:S(2)}) collective-permute-start(f32[12,128]{1,0:T(8,128)S(1)} %get-tuple-element.23), channel_id=1, source_target_pairs={{0,14},{1,15},{2,4},{3,5},{4,2},{5,3},{6,8},{7,9},{8,6},{9,7},{10,... | collective-permute-start | bytes 18440 | tf_op jit(solution)/shard_map/ppermute | solution.py:207
  51.2 4.2 %collective-permute-start.12 = (f32[48,128]{1,0:T(8,128)S(1)}, f32[48,128]{1,0:T(8,128)S(1)}, u32[]{:S(2)}, u32[]{:S(2)}) collective-permute-start(f32[48,128]{1,0:T(8,128)S(1)} %get-tuple-element.7), channel_id=1, source_target_pairs={{0,16},{16,0},{32,48},{48,32},{64,80},{80,64},{96,112},{112,96},{1... | collective-permute-start | bytes 73736 | tf_op jit(solution)/shard_map/ppermute | solution.py:207
  52.9 6.9 %collective-permute-start.13 = (f32[48,128]{1,0:T(8,128)S(1)}, f32[48,128]{1,0:T(8,128)S(1)}, u32[]{:S(2)}, u32[]{:S(2)}) collective-permute-start(f32[48,128]{1,0:T(8,128)S(1)} %get-tuple-element.8), channel_id=1, source_target_pairs={{0,240},{16,32},{32,16},{48,64},{64,48},{80,96},{96,80},{112,128},... | collective-permute-start | bytes 73736 | tf_op jit(solution)/shard_map/ppermute | solution.py:207
  59.8 4.3 %collective-permute-start.14 = (f32[16,128]{1,0:T(8,128)S(1)}, f32[16,128]{1,0:T(8,128)S(1)}, u32[]{:S(2)}, u32[]{:S(2)}) collective-permute-start(f32[16,128]{1,0:T(8,128)S(1)} %get-tuple-element.12), channel_id=1, source_target_pairs={{0,1},{1,0},{2,3},{3,2},{4,5},{5,4},{6,7},{7,6},{8,9},{9,8},{10,11... | collective-permute-start | bytes 24584 | tf_op jit(solution)/shard_map/ppermute | solution.py:207
  63.3 3.1 %collective-permute-start.15 = (f32[16,128]{1,0:T(8,128)S(1)}, f32[16,128]{1,0:T(8,128)S(1)}, u32[]{:S(2)}, u32[]{:S(2)}) collective-permute-start(f32[16,128]{1,0:T(8,128)S(1)} %get-tuple-element.13), channel_id=1, source_target_pairs={{0,15},{1,2},{2,1},{3,4},{4,3},{5,6},{6,5},{7,8},{8,7},{9,10},{10,... | collective-permute-start | bytes 24584 | tf_op jit(solution)/shard_map/ppermute | solution.py:207

commit v3 on v2

--- a/solution.py
+++ b/solution.py
@@ -43,8 +43,8 @@
 
 def along_sites(left, right):
     return lax.dot_general(
-        left, right, (((1,), (1,)), ((), ())), preferred_element_type=jnp.float32
-    )
+        right, left, (((1,), (1,)), ((), ())), preferred_element_type=jnp.float32
+    ).T
 
 
 def along_points(left, right):
@@ -115,7 +115,7 @@
                     d_ref[2 * g, rows, lanes], d_ref[2 * g + 1, rows, lanes] = halves(e * dz)
         return carry
 
-    lax.fori_loop(0, Z // CHUNK, visit, 0)
+    lax.fori_loop(0, Z // CHUNK, visit, 0, unroll=True)
 
     point = lax.broadcasted_iota(jnp.int32, (HALF, SITES), 0)
     at_y = (point % TY).astype(jnp.float32) + 0.5
@@ -192,6 +192,41 @@
     )(*given)
 
 
+def pack_kernel(frac_ref, weight_ref, target_ref, out_ref):
+    for x in range(SIDE):
+        for c in range(3):
+            out_ref[pl.ds(c * INNER + x * SIDE, SIDE), :] = frac_ref[c, x]
+        out_ref[pl.ds(3 * INNER + x * SIDE, SIDE), :] = weight_ref[x]
+        out_ref[pl.ds(4 * INNER + x * SIDE, SIDE), :] = target_ref[x]
+    out_ref[pl.ds(5 * INNER, FIELDS - 5 * INNER), :] = jnp.zeros((FIELDS - 5 * INNER, BLOCK), jnp.float32)
+
+
+def finish_kernel(tile_ref, masses_ref, own_ref, even_ref, odd_ref, dual_ref, shift_ref):
+    sums = own_ref[4 * INNER : 8 * INNER] + even_ref[...] + odd_ref[...]
+    weight, target = tile_ref[3 * INNER : 4 * INNER], tile_ref[4 * INNER : 5 * INNER]
+    mid = weight + step_rate * (target - masses_ref[4 * INNER : 5 * INNER])
+    dual = mid + step_rate * (target - sums[:INNER])
+    share = sums[:INNER] + target
+    for x in range(SIDE):
+        rows = slice(x * SIDE, (x + 1) * SIDE)
+        dual_ref[x] = dual[rows]
+        for c in range(3):
+            moment = sums[(c + 1) * INNER : (c + 2) * INNER]
+            shift_ref[c, x] = (moment / share)[rows]
+
+
+def run_small(kernel, shapes, *given):
+    vmem = pl.BlockSpec(memory_space=pltpu.VMEM)
+    shapes = jax.tree.map(lambda shape: jax.ShapeDtypeStruct(shape, jnp.float32), shapes, is_leaf=lambda s: type(s[0]) is int)
+    return pl.pallas_call(
+        kernel,
+        out_shape=shapes,
+        in_specs=[vmem] * len(given),
+        out_specs=jax.tree.map(lambda _: vmem, shapes),
+        compiler_params=pltpu.CompilerParams(vmem_limit_bytes=4 * 2**20),
+    )(*given)
+
+
 def partner(kind, i, peers):
     if kind == "even":
         return i ^ 1
@@ -241,17 +276,7 @@
     ids = jnp.concatenate(
         [block_list.reshape(K_MAX), block_count.reshape(1), jnp.stack(ways).astype(jnp.int32)]
     )
-    weight = dual_weight.reshape(INNER, BLOCK)
-    target = target_mass.reshape(INNER, BLOCK)
-    tile = jnp.concatenate(
-        [
-            site_frac.reshape(3 * INNER, BLOCK),
-            weight,
-            target,
-            jnp.zeros((FIELDS - 5 * INNER, BLOCK), jnp.float32),
-        ],
-        0,
-    )
+    tile = run_small(pack_kernel, (FIELDS, BLOCK), site_frac, dual_weight, target_mass)
     table = with_sides(with_sides(tile, "gx"), "gy")
 
     partial = run_pass(ids, table)
@@ -262,16 +287,13 @@
     masses = jnp.concatenate(folded_with_sides(rims, "gy"), 0)
 
     spread, displacement = run_pass(ids, table, masses)
-    sums = folded(folded(spread, "gx"), "gy")
-    mass = sums[:INNER]
-    mid = weight + step_rate * (target - masses[4 * INNER : 5 * INNER])
-    new_dual = mid + step_rate * (target - mass)
-    site_shift = sums[INNER:].reshape(3, INNER, BLOCK) / (mass + target)[None]
-    return (
-        new_dual.reshape(SIDE, SIDE, BLOCK),
-        site_shift.reshape(3, SIDE, SIDE, BLOCK),
-        displacement,
-    )
+    column = folded(spread, "gx")
+    even = swapped(column[: 4 * INNER], "gy", "even")
+    odd = swapped(column[8 * INNER :], "gy", "odd")
+    new_dual, site_shift = run_small(
+        finish_kernel, (dual_weight.shape, site_frac.shape), tile, masses, column, even, odd
+    )
+    return new_dual, site_shift, displacement
 
 
 def solution(mesh):

time: 67.8 us -> 64.7 us (0.954)
  starting transfers between devices: 35.8 us -> 32.7 us
  waiting for transfers between devices: 15.8 us -> 18.2 us
  Pallas kernels: 11 us -> 8.78 us
  other arithmetic: 1.35 us -> 0.15 us
    ppermute x16, starting transfers between devices: 35.8 us -> 32.7 us  [swapped(): lax.ppermute(array, axis, [(i, partner(kind, i, peers)) for i in range(pe...]
    pallas_call x2, Pallas kernels: 11 us -> 8.17 us  [run_pass(): pl.pallas_call(functools.partial(pass_kernel, moments), out_shape=shapes,...]
    ppermute x16, waiting for transfers between devices: 15.8 us -> 18.2 us  [swapped(): lax.ppermute(array, axis, [(i, partner(kind, i, peers)) for i in range(pe...]
    unnamed x6 -> x12, local copies, waits for them, and re-layouts: 1.34 us -> 2.71 us
    reshape x2 -> x0, local copies, waits for them, and re-layouts: 0.71 us -> none  [the longest x1 0.7 us: on_device(): site_frac.reshape(3 * INNER, BLOCK)]
  transfers between devices with their start and end apart: 16 -> 16, of which waited for: 10 -> 9; matrix products, arithmetic and copies ran while one was open for 0% -> 0% of each run, Pallas kernels for 0% -> 0%
where the time goes in v3:
time: 64.7 us; the launch traced here: 64.1 us
  starting transfers between devices  32.7 us (51%)
  waiting for transfers between devices  18.2 us (28%)
  Pallas kernels  8.78 us (14%)
  local copies, waits for them, and re-layouts  2.86 us (4%)
  between operations  1.39 us (2%)
    ppermute x16, starting transfers between devices, swapped(): lax.ppermute(array, axis, [(i, partner(kind, i, peers)) for i in range(pe...  32.7 us
    ppermute x16, waiting for transfers between devices, swapped(): lax.ppermute(array, axis, [(i, partner(kind, i, peers)) for i in range(pe...  18.2 us
    pallas_call x2, Pallas kernels, run_pass(): pl.pallas_call(functools.partial(pass_kernel, moments), out_shape=shapes,...  8.17 us
    unnamed x12, local copies, waits for them, and re-layouts  2.71 us
  transfers between devices with their start and end apart: 16, of which 9 were waited for; matrix products, arithmetic and copies ran while one was open for 0% of the time, Pallas kernels for 0%

profile of v3, /device:TPU:1, one launch (start us, length us, event | category | flops | bytes accessed | tf_op | source)
XLA Modules:
  0.0 64.1 jit_solution(17393220567776538501)
XLA Ops:
  0.6 0.7 %copy-done = f32[3,2,2,128]{3,2,1,0:T(2,128)S(1)} copy-done((f32[3,2,2,128]{3,2,1,0:T(2,128)S(1)}, f32[3,2,2,128]{3,2,1,0:T(2,128)}, u32[]{:S(2)}) %copy-start) | copy-done | bytes 6168
  1.3 0.7 %copy-done.1 = f32[2,2,128]{2,1,0:T(2,128)S(1)} copy-done((f32[2,2,128]{2,1,0:T(2,128)S(1)}, f32[2,2,128]{2,1,0:T(2,128)}, u32[]{:S(2)}) %copy-start.1) | copy-done | bytes 2072
  2.0 0.7 %copy-done.2 = f32[2,2,128]{2,1,0:T(2,128)S(1)} copy-done((f32[2,2,128]{2,1,0:T(2,128)S(1)}, f32[2,2,128]{2,1,0:T(2,128)}, u32[]{:S(2)}) %copy-start.2) | copy-done | bytes 2072
  2.7 9.0 %collective-permute-start.1 = (f32[24,128]{1,0:T(8,128)S(1)}, f32[24,128]{1,0:T(8,128)S(1)}, u32[]{:S(2)}, u32[]{:S(2)}) collective-permute-start(f32[24,128]{1,0:T(8,128)S(1)} %shard_map.76.tile_ref), channel_id=1, source_target_pairs={{0,240},{16,32},{32,16},{48,64},{64,48},{80,96},{96,80},{112,128},... | collective-permute-start | bytes 36872 | tf_op jit(solution)/shard_map/ppermute | solution.py:242
  11.7 0.0 collective-permute-start
  12.4 0.4 collective-permute-done.1
  12.8 1.5 %collective-permute-done = f32[24,128]{1,0:T(8,128)S(1)} collective-permute-done((f32[24,128]{1,0:T(8,128)S(1)}, f32[24,128]{1,0:T(8,128)S(1)}, u32[]{:S(2)}, u32[]{:S(2)}) %collective-permute-start) | collective-permute-done | bytes 12320 | tf_op jit(solution)/shard_map/ppermute | solution.py:242
  14.3 2.1 %collective-permute-start.2 = (f32[72,128]{1,0:T(8,128)S(1)}, f32[72,128]{1,0:T(8,128)S(1)}, u32[]{:S(2)}, u32[]{:S(2)}) collective-permute-start(f32[72,128]{1,0:T(8,128)S(1)} %pad_maximum_fusion), channel_id=1, source_target_pairs={{0,1},{1,0},{2,3},{3,2},{4,5},{5,4},{6,7},{7,6},{8,9},{9,8},{10,11... | collective-permute-start | bytes 110600 | tf_op jit(solution)/shard_map/ppermute | solution.py:242
  16.4 0.7 %copy-done.3 = s32[1,1,12]{2,1,0:T(1,128)S(1)} copy-done((s32[1,1,12]{2,1,0:T(1,128)S(1)}, s32[1,1,12]{2,1,0:T(1,128)}, u32[]{:S(2)}) %copy-start.3) | copy-done | bytes 72
  17.1 0.1 pad_add_fusion.ids_ref
  17.1 0.7 %collective-permute-start.3 = (f32[72,128]{1,0:T(8,128)S(1)}, f32[72,128]{1,0:T(8,128)S(1)}, u32[]{:S(2)}, u32[]{:S(2)}) collective-permute-start(f32[72,128]{1,0:T(8,128)S(1)} %pad_maximum_fusion), channel_id=1, source_target_pairs={{0,15},{1,2},{2,1},{3,4},{4,3},{5,6},{6,5},{7,8},{8,7},{9,10},{10,... | collective-permute-start | bytes 110600 | tf_op jit(solution)/shard_map/ppermute | solution.py:242
  17.8 2.8 %collective-permute-done.3 = f32[72,128]{1,0:T(8,128)S(1)} collective-permute-done((f32[72,128]{1,0:T(8,128)S(1)}, f32[72,128]{1,0:T(8,128)S(1)}, u32[]{:S(2)}, u32[]{:S(2)}) %collective-permute-start.3) | collective-permute-done | bytes 36896 | tf_op jit(solution)/shard_map/ppermute | solution.py:242
  20.6 3.4 %shard_map.77 = f32[48,128]{1,0:T(8,128)S(1)} custom-call(s32[15]{0:T(128)S(1)} %pad_add_fusion.ids_ref, f32[216,128]{1,0:T(8,128)S(1)} %constant_dynamic-update-slice_fusion.table_ref), custom_call_target="tpu_custom_call" | custom-call | tf_op jit(solution)/shard_map/pallas_call | solution.py:185
  24.0 4.1 %collective-permute-start.7 = (f32[24,128]{1,0:T(8,128)S(1)}, f32[24,128]{1,0:T(8,128)S(1)}, u32[]{:S(2)}, u32[]{:S(2)}) collective-permute-start(f32[24,128]{1,0:T(8,128)S(1)} %get-tuple-element.37), channel_id=1, source_target_pairs={{0,240},{16,32},{32,16},{48,64},{64,48},{80,96},{96,80},{112,128},... | collective-permute-start | bytes 36872 | tf_op jit(solution)/shard_map/ppermute | solution.py:242
  28.1 2.9 %collective-permute-start.6 = (f32[12,128]{1,0:T(8,128)S(1)}, f32[12,128]{1,0:T(8,128)S(1)}, u32[]{:S(2)}, u32[]{:S(2)}) collective-permute-start(f32[12,128]{1,0:T(8,128)S(1)} %get-tuple-element.20), channel_id=1, source_target_pairs={{0,224},{16,240},{32,64},{48,80},{64,32},{80,48},{96,128},{112,144... | collective-permute-start | bytes 18440 | tf_op jit(solution)/shard_map/ppermute | solution.py:242
  31.0 1.1 %collective-permute-done.5 = f32[12,128]{1,0:T(8,128)S(1)} collective-permute-done((f32[12,128]{1,0:T(8,128)S(1)}, f32[12,128]{1,0:T(8,128)S(1)}, u32[]{:S(2)}, u32[]{:S(2)}) %collective-permute-start.5) | collective-permute-done | bytes 6176 | tf_op jit(solution)/shard_map/ppermute | solution.py:242
  32.1 3.0 %collective-permute-done.6 = f32[12,128]{1,0:T(8,128)S(1)} collective-permute-done((f32[12,128]{1,0:T(8,128)S(1)}, f32[12,128]{1,0:T(8,128)S(1)}, u32[]{:S(2)}, u32[]{:S(2)}) %collective-permute-start.6) | collective-permute-done | bytes 6176 | tf_op jit(solution)/shard_map/ppermute | solution.py:242
  35.2 0.1 concatenate.45
  35.3 2.1 %collective-permute-start.11 = (f32[24,128]{1,0:T(8,128)S(1)}, f32[24,128]{1,0:T(8,128)S(1)}, u32[]{:S(2)}, u32[]{:S(2)}) collective-permute-start(f32[24,128]{1,0:T(8,128)S(1)} %concatenate.45), channel_id=1, source_target_pairs={{0,15},{1,2},{2,1},{3,4},{4,3},{5,6},{6,5},{7,8},{8,7},{9,10},{10,... | collective-permute-start | bytes 36872 | tf_op jit(solution)/shard_map/ppermute | solution.py:242
  37.3 0.1 concatenate.41
  37.4 3.7 %collective-permute-start.8 = (f32[24,128]{1,0:T(8,128)S(1)}, f32[24,128]{1,0:T(8,128)S(1)}, u32[]{:S(2)}, u32[]{:S(2)}) collective-permute-start(f32[24,128]{1,0:T(8,128)S(1)} %concatenate.41), channel_id=1, source_target_pairs={{0,1},{1,0},{2,3},{3,2},{4,5},{5,4},{6,7},{7,6},{8,9},{9,8},{10,11... | collective-permute-start | bytes 36872 | tf_op jit(solution)/shard_map/ppermute | solution.py:242
  41.1 0.1 collective-permute-start.9
  41.2 1.6 %collective-permute-start.10 = (f32[12,128]{1,0:T(8,128)S(1)}, f32[12,128]{1,0:T(8,128)S(1)}, u32[]{:S(2)}, u32[]{:S(2)}) collective-permute-start(f32[12,128]{1,0:T(8,128)S(1)} %get-tuple-element.27), channel_id=1, source_target_pairs={{0,14},{1,15},{2,4},{3,5},{4,2},{5,3},{6,8},{7,9},{8,6},{9,7},{10,... | collective-permute-start | bytes 18440 | tf_op jit(solution)/shard_map/ppermute | solution.py:242
  42.8 0.9 %collective-permute-done.9 = f32[12,128]{1,0:T(8,128)S(1)} collective-permute-done((f32[12,128]{1,0:T(8,128)S(1)}, f32[12,128]{1,0:T(8,128)S(1)}, u32[]{:S(2)}, u32[]{:S(2)}) %collective-permute-start.9) | collective-permute-done | bytes 6176 | tf_op jit(solution)/shard_map/ppermute | solution.py:242
  43.7 2.4 %collective-permute-done.10 = f32[12,128]{1,0:T(8,128)S(1)} collective-permute-done((f32[12,128]{1,0:T(8,128)S(1)}, f32[12,128]{1,0:T(8,128)S(1)}, u32[]{:S(2)}, u32[]{:S(2)}) %collective-permute-start.10) | collective-permute-done | bytes 6176 | tf_op jit(solution)/shard_map/ppermute | solution.py:242
  46.1 4.8 %shard_map.78 = (f32[144,128]{1,0:T(8,128)S(1)}, f32[3,4,4,256]{3,2,1,0:T(4,128)}) custom-call(s32[15]{0:T(128)S(1)} %pad_add_fusion.ids_ref, f32[216,128]{1,0:T(8,128)S(1)} %constant_dynamic-update-slice_fusion.table_ref, f32[36,128]{1,0:T(8,128)S(1)} %pad_maximum_fusion.1.refs_0_.masses_ref), custom_call_target="tpu_custom_call" | custom-call | tf_op jit(solution)/shard_map/pallas_call | solution.py:185
  50.9 1.5 %collective-permute-start.12 = (f32[48,128]{1,0:T(8,128)S(1)}, f32[48,128]{1,0:T(8,128)S(1)}, u32[]{:S(2)}, u32[]{:S(2)}) collective-permute-start(f32[48,128]{1,0:T(8,128)S(1)} %get-tuple-element.11), channel_id=1, source_target_pairs={{0,16},{16,0},{32,48},{48,32},{64,80},{80,64},{96,112},{112,96},{1... | collective-permute-start | bytes 73736 | tf_op jit(solution)/shard_map/ppermute | solution.py:242
  52.4 2.2 %collective-permute-start.13 = (f32[48,128]{1,0:T(8,128)S(1)}, f32[48,128]{1,0:T(8,128)S(1)}, u32[]{:S(2)}, u32[]{:S(2)}) collective-permute-start(f32[48,128]{1,0:T(8,128)S(1)} %get-tuple-element.12), channel_id=1, source_target_pairs={{0,240},{16,32},{32,16},{48,64},{64,48},{80,96},{96,80},{112,128},... | collective-permute-start | bytes 73736 | tf_op jit(solution)/shard_map/ppermute | solution.py:242
  54.6 4.7 %collective-permute-done.13 = f32[48,128]{1,0:T(8,128)S(1)} collective-permute-done((f32[48,128]{1,0:T(8,128)S(1)}, f32[48,128]{1,0:T(8,128)S(1)}, u32[]{:S(2)}, u32[]{:S(2)}) %collective-permute-start.13) | collective-permute-done | bytes 24608 | tf_op jit(solution)/shard_map/ppermute | solution.py:242
  59.3 2.8 %collective-permute-start.15 = (f32[16,128]{1,0:T(8,128)S(1)}, f32[16,128]{1,0:T(8,128)S(1)}, u32[]{:S(2)}, u32[]{:S(2)}) collective-permute-start(f32[16,128]{1,0:T(8,128)S(1)} %get-tuple-element.16), channel_id=1, source_target_pairs={{0,15},{1,2},{2,1},{3,4},{4,3},{5,6},{6,5},{7,8},{8,7},{9,10},{10,... | collective-permute-start | bytes 24584 | tf_op jit(solution)/shard_map/ppermute | solution.py:242
  62.1 1.3 %collective-permute-done.15.odd_ref = f32[16,128]{1,0:T(8,128)S(1)} collective-permute-done((f32[16,128]{1,0:T(8,128)S(1)}, f32[16,128]{1,0:T(8,128)S(1)}, u32[]{:S(2)}, u32[]{:S(2)}) %collective-permute-start.15) | collective-permute-done | bytes 8224 | tf_op jit(solution)/shard_map/ppermute | solution.py:242
  63.5 0.6 shard_map.79
  (32 shorter events, 0.1 us)
Async XLA Ops:
  0.6 0.7 %copy-start = (f32[3,2,2,128]{3,2,1,0:T(2,128)S(1)}, f32[3,2,2,128]{3,2,1,0:T(2,128)}, u32[]{:S(2)}) copy-start(f32[3,2,2,128]{3,2,1,0:T(2,128)} %frac_ref.1) | copy-start | bytes 18436
  1.3 0.7 %copy-start.1 = (f32[2,2,128]{2,1,0:T(2,128)S(1)}, f32[2,2,128]{2,1,0:T(2,128)}, u32[]{:S(2)}) copy-start(f32[2,2,128]{2,1,0:T(2,128)} %weight_ref.1) | copy-start | bytes 6148
  2.0 0.7 %copy-start.2 = (f32[2,2,128]{2,1,0:T(2,128)S(1)}, f32[2,2,128]{2,1,0:T(2,128)}, u32[]{:S(2)}) copy-start(f32[2,2,128]{2,1,0:T(2,128)} %target_ref.1) | copy-start | bytes 6148
  2.7 10.1 %collective-permute-start.1 = (f32[24,128]{1,0:T(8,128)S(1)}, f32[24,128]{1,0:T(8,128)S(1)}, u32[]{:S(2)}, u32[]{:S(2)}) collective-permute-start(f32[24,128]{1,0:T(8,128)S(1)} %shard_map.76.tile_ref), channel_id=1, source_target_pairs={{0,240},{16,32},{32,16},{48,64},{64,48},{80,96},{96,80},{112,128},... | collective-permute-start | bytes 36872 | tf_op jit(solution)/shard_map/ppermute | solution.py:242
  11.7 2.5 %collective-permute-start = (f32[24,128]{1,0:T(8,128)S(1)}, f32[24,128]{1,0:T(8,128)S(1)}, u32[]{:S(2)}, u32[]{:S(2)}) collective-permute-start(f32[24,128]{1,0:T(8,128)S(1)} %shard_map.76.tile_ref), channel_id=1, source_target_pairs={{0,16},{16,0},{32,48},{48,32},{64,80},{80,64},{96,112},{112,96},{1... | collective-permute-start | bytes 36872 | tf_op jit(solution)/shard_map/ppermute | solution.py:242
  14.3 3.5 %collective-permute-start.2 = (f32[72,128]{1,0:T(8,128)S(1)}, f32[72,128]{1,0:T(8,128)S(1)}, u32[]{:S(2)}, u32[]{:S(2)}) collective-permute-start(f32[72,128]{1,0:T(8,128)S(1)} %pad_maximum_fusion), channel_id=1, source_target_pairs={{0,1},{1,0},{2,3},{3,2},{4,5},{5,4},{6,7},{7,6},{8,9},{9,8},{10,11... | collective-permute-start | bytes 110600 | tf_op jit(solution)/shard_map/ppermute | solution.py:242
  16.4 0.7 %copy-start.3 = (s32[1,1,12]{2,1,0:T(1,128)S(1)}, s32[1,1,12]{2,1,0:T(1,128)}, u32[]{:S(2)}) copy-start(s32[1,1,12]{2,1,0:T(1,128)} %param.8) | copy-start | bytes 148
  17.1 3.5 %collective-permute-start.3 = (f32[72,128]{1,0:T(8,128)S(1)}, f32[72,128]{1,0:T(8,128)S(1)}, u32[]{:S(2)}, u32[]{:S(2)}) collective-permute-start(f32[72,128]{1,0:T(8,128)S(1)} %pad_maximum_fusion), channel_id=1, source_target_pairs={{0,15},{1,2},{2,1},{3,4},{4,3},{5,6},{6,5},{7,8},{8,7},{9,10},{10,... | collective-permute-start | bytes 110600 | tf_op jit(solution)/shard_map/ppermute | solution.py:242
  24.0 11.1 %collective-permute-start.7 = (f32[24,128]{1,0:T(8,128)S(1)}, f32[24,128]{1,0:T(8,128)S(1)}, u32[]{:S(2)}, u32[]{:S(2)}) collective-permute-start(f32[24,128]{1,0:T(8,128)S(1)} %get-tuple-element.37), channel_id=1, source_target_pairs={{0,240},{16,32},{32,16},{48,64},{64,48},{80,96},{96,80},{112,128},... | collective-permute-start | bytes 36872 | tf_op jit(solution)/shard_map/ppermute | solution.py:242
  28.1 7.0 %collective-permute-start.4 = (f32[24,128]{1,0:T(8,128)S(1)}, f32[24,128]{1,0:T(8,128)S(1)}, u32[]{:S(2)}, u32[]{:S(2)}) collective-permute-start(f32[24,128]{1,0:T(8,128)S(1)} %get-tuple-element.38), channel_id=1, source_target_pairs={{0,16},{16,0},{32,48},{48,32},{64,80},{80,64},{96,112},{112,96},{1... | collective-permute-start | bytes 36872 | tf_op jit(solution)/shard_map/ppermute | solution.py:242
  28.1 4.0 %collective-permute-start.5 = (f32[12,128]{1,0:T(8,128)S(1)}, f32[12,128]{1,0:T(8,128)S(1)}, u32[]{:S(2)}, u32[]{:S(2)}) collective-permute-start(f32[12,128]{1,0:T(8,128)S(1)} %get-tuple-element.19), channel_id=1, source_target_pairs={{0,32},{16,48},{32,0},{48,16},{64,96},{80,112},{96,64},{112,80},{1... | collective-permute-start | bytes 18440 | tf_op jit(solution)/shard_map/ppermute | solution.py:242
  28.1 7.0 %collective-permute-start.6 = (f32[12,128]{1,0:T(8,128)S(1)}, f32[12,128]{1,0:T(8,128)S(1)}, u32[]{:S(2)}, u32[]{:S(2)}) collective-permute-start(f32[12,128]{1,0:T(8,128)S(1)} %get-tuple-element.20), channel_id=1, source_target_pairs={{0,224},{16,240},{32,64},{48,80},{64,32},{80,48},{96,128},{112,144... | collective-permute-start | bytes 18440 | tf_op jit(solution)/shard_map/ppermute | solution.py:242
  35.3 10.8 %collective-permute-start.11 = (f32[24,128]{1,0:T(8,128)S(1)}, f32[24,128]{1,0:T(8,128)S(1)}, u32[]{:S(2)}, u32[]{:S(2)}) collective-permute-start(f32[24,128]{1,0:T(8,128)S(1)} %concatenate.45), channel_id=1, source_target_pairs={{0,15},{1,2},{2,1},{3,4},{4,3},{5,6},{6,5},{7,8},{8,7},{9,10},{10,... | collective-permute-start | bytes 36872 | tf_op jit(solution)/shard_map/ppermute | solution.py:242
  37.4 8.7 %collective-permute-start.8 = (f32[24,128]{1,0:T(8,128)S(1)}, f32[24,128]{1,0:T(8,128)S(1)}, u32[]{:S(2)}, u32[]{:S(2)}) collective-permute-start(f32[24,128]{1,0:T(8,128)S(1)} %concatenate.41), channel_id=1, source_target_pairs={{0,1},{1,0},{2,3},{3,2},{4,5},{5,4},{6,7},{7,6},{8,9},{9,8},{10,11... | collective-permute-start | bytes 36872 | tf_op jit(solution)/shard_map/ppermute | solution.py:242
  41.1 2.6 %collective-permute-start.9 = (f32[12,128]{1,0:T(8,128)S(1)}, f32[12,128]{1,0:T(8,128)S(1)}, u32[]{:S(2)}, u32[]{:S(2)}) collective-permute-start(f32[12,128]{1,0:T(8,128)S(1)} %get-tuple-element.26), channel_id=1, source_target_pairs={{0,2},{1,3},{2,0},{3,1},{4,6},{5,7},{6,4},{7,5},{8,10},{9,11},{10,... | collective-permute-start | bytes 18440 | tf_op jit(solution)/shard_map/ppermute | solution.py:242
  41.2 4.9 %collective-permute-start.10 = (f32[12,128]{1,0:T(8,128)S(1)}, f32[12,128]{1,0:T(8,128)S(1)}, u32[]{:S(2)}, u32[]{:S(2)}) collective-permute-start(f32[12,128]{1,0:T(8,128)S(1)} %get-tuple-element.27), channel_id=1, source_target_pairs={{0,14},{1,15},{2,4},{3,5},{4,2},{5,3},{6,8},{7,9},{8,6},{9,7},{10,... | collective-permute-start | bytes 18440 | tf_op jit(solution)/shard_map/ppermute | solution.py:242
  50.9 3.6 %collective-permute-start.12 = (f32[48,128]{1,0:T(8,128)S(1)}, f32[48,128]{1,0:T(8,128)S(1)}, u32[]{:S(2)}, u32[]{:S(2)}) collective-permute-start(f32[48,128]{1,0:T(8,128)S(1)} %get-tuple-element.11), channel_id=1, source_target_pairs={{0,16},{16,0},{32,48},{48,32},{64,80},{80,64},{96,112},{112,96},{1... | collective-permute-start | bytes 73736 | tf_op jit(solution)/shard_map/ppermute | solution.py:242
  52.4 6.9 %collective-permute-start.13 = (f32[48,128]{1,0:T(8,128)S(1)}, f32[48,128]{1,0:T(8,128)S(1)}, u32[]{:S(2)}, u32[]{:S(2)}) collective-permute-start(f32[48,128]{1,0:T(8,128)S(1)} %get-tuple-element.12), channel_id=1, source_target_pairs={{0,240},{16,32},{32,16},{48,64},{64,48},{80,96},{96,80},{112,128},... | collective-permute-start | bytes 73736 | tf_op jit(solution)/shard_map/ppermute | solution.py:242
  59.3 4.1 %collective-permute-start.15 = (f32[16,128]{1,0:T(8,128)S(1)}, f32[16,128]{1,0:T(8,128)S(1)}, u32[]{:S(2)}, u32[]{:S(2)}) collective-permute-start(f32[16,128]{1,0:T(8,128)S(1)} %get-tuple-element.16), channel_id=1, source_target_pairs={{0,15},{1,2},{2,1},{3,4},{4,3},{5,6},{6,5},{7,8},{8,7},{9,10},{10,... | collective-permute-start | bytes 24584 | tf_op jit(solution)/shard_map/ppermute | solution.py:242
  62.1 1.3 %collective-permute-start.14 = (f32[16,128]{1,0:T(8,128)S(1)}, f32[16,128]{1,0:T(8,128)S(1)}, u32[]{:S(2)}, u32[]{:S(2)}) collective-permute-start(f32[16,128]{1,0:T(8,128)S(1)} %get-tuple-element.17), channel_id=1, source_target_pairs={{0,1},{1,0},{2,3},{3,2},{4,5},{5,4},{6,7},{7,6},{8,9},{9,8},{10,11... | collective-permute-start | bytes 24584 | tf_op jit(solution)/shard_map/ppermute | solution.py:242

commit v4 on v3

--- a/solution.py
+++ b/solution.py
@@ -24,7 +24,7 @@
 SCALE = 2.0**-20
 NEVER = -1.0e7
 
-FIELDS = 24
+FIELDS = 5
 ROWS = 16
 CHUNK = 64
 
@@ -66,19 +66,24 @@
         slot = ids_ref[m]
         row, col = slot // (3 * SIDE), slot % (3 * SIDE)
         tx, ty = row // SIDE, col // SIDE
-        inner = row % SIDE * SIDE + col % SIDE
+        place_x, place_y = row % SIDE, col % SIDE
+        inner = place_x * SIDE + place_y
         bx, by = 1 + (tx - 1) * way_x, 1 + (ty - 1) * way_y
         places.append((bx, by, inner))
-        base = (by * 3 + bx) * FIELDS + inner
+        base = (by * 3 + bx) * FIELDS
+
+        def field(f):
+            return table_ref[base + f, place_x, pl.ds(place_y, 1), :]
+
         off_x = ((tx - 1) * TX).astype(jnp.float32)
         off_y = ((ty - 1) * TY).astype(jnp.float32)
         lanes = pl.ds(m * BLOCK, BLOCK)
-        site_ref[0:1, lanes] = table_ref[pl.ds(base, 1), :] * TX + off_x
-        site_ref[1:2, lanes] = table_ref[pl.ds(base + INNER, 1), :] * TY + off_y
-        site_ref[2:3, lanes] = table_ref[pl.ds(base + 2 * INNER, 1), :] * Z
-        weight = table_ref[pl.ds(base + 3 * INNER, 1), :]
+        site_ref[0:1, lanes] = field(0) * TX + off_x
+        site_ref[1:2, lanes] = field(1) * TY + off_y
+        site_ref[2:3, lanes] = field(2) * Z
+        weight = field(3)
         if moments:
-            goal = table_ref[pl.ds(base + 4 * INNER, 1), :]
+            goal = field(4)
             mass = mass_ref[pl.ds((by * 3 + bx) * INNER + inner, 1), :]
             weight = weight + step_rate * (goal - mass)
         site_ref[3:4, lanes] = jnp.where(m < count, weight, NEVER)
@@ -192,37 +197,26 @@
     )(*given)
 
 
-def pack_kernel(frac_ref, weight_ref, target_ref, out_ref):
-    for x in range(SIDE):
-        for c in range(3):
-            out_ref[pl.ds(c * INNER + x * SIDE, SIDE), :] = frac_ref[c, x]
-        out_ref[pl.ds(3 * INNER + x * SIDE, SIDE), :] = weight_ref[x]
-        out_ref[pl.ds(4 * INNER + x * SIDE, SIDE), :] = target_ref[x]
-    out_ref[pl.ds(5 * INNER, FIELDS - 5 * INNER), :] = jnp.zeros((FIELDS - 5 * INNER, BLOCK), jnp.float32)
-
-
 def finish_kernel(tile_ref, masses_ref, own_ref, even_ref, odd_ref, dual_ref, shift_ref):
     sums = own_ref[4 * INNER : 8 * INNER] + even_ref[...] + odd_ref[...]
-    weight, target = tile_ref[3 * INNER : 4 * INNER], tile_ref[4 * INNER : 5 * INNER]
-    mid = weight + step_rate * (target - masses_ref[4 * INNER : 5 * INNER])
-    dual = mid + step_rate * (target - sums[:INNER])
-    share = sums[:INNER] + target
     for x in range(SIDE):
         rows = slice(x * SIDE, (x + 1) * SIDE)
-        dual_ref[x] = dual[rows]
+        mass, target = sums[rows], tile_ref[4, x]
+        first = masses_ref[4 * INNER + x * SIDE : 4 * INNER + (x + 1) * SIDE]
+        mid = tile_ref[3, x] + step_rate * (target - first)
+        dual_ref[x] = mid + step_rate * (target - mass)
         for c in range(3):
             moment = sums[(c + 1) * INNER : (c + 2) * INNER]
-            shift_ref[c, x] = (moment / share)[rows]
-
-
-def run_small(kernel, shapes, *given):
+            shift_ref[c, x] = moment[rows] / (mass + target)
+
+
+def run_finish(like_dual, like_shift, *given):
     vmem = pl.BlockSpec(memory_space=pltpu.VMEM)
-    shapes = jax.tree.map(lambda shape: jax.ShapeDtypeStruct(shape, jnp.float32), shapes, is_leaf=lambda s: type(s[0]) is int)
     return pl.pallas_call(
-        kernel,
-        out_shape=shapes,
+        finish_kernel,
+        out_shape=tuple(jax.ShapeDtypeStruct(a.shape, jnp.float32) for a in (like_dual, like_shift)),
         in_specs=[vmem] * len(given),
-        out_specs=jax.tree.map(lambda _: vmem, shapes),
+        out_specs=(vmem, vmem),
         compiler_params=pltpu.CompilerParams(vmem_limit_bytes=4 * 2**20),
     )(*given)
 
@@ -276,8 +270,11 @@
     ids = jnp.concatenate(
         [block_list.reshape(K_MAX), block_count.reshape(1), jnp.stack(ways).astype(jnp.int32)]
     )
-    tile = run_small(pack_kernel, (FIELDS, BLOCK), site_frac, dual_weight, target_mass)
-    table = with_sides(with_sides(tile, "gx"), "gy")
+    tile = lax.optimization_barrier(
+        jnp.concatenate([site_frac, dual_weight[None], target_mass[None]], 0)
+    )
+    column, ids = lax.optimization_barrier((with_sides(tile, "gx"), ids))
+    table = with_sides(column, "gy")
 
     partial = run_pass(ids, table)
     blocks = folded_with_sides([partial[i * ROWS : i * ROWS + 3 * INNER] for i in range(3)], "gx")
@@ -287,11 +284,11 @@
     masses = jnp.concatenate(folded_with_sides(rims, "gy"), 0)
 
     spread, displacement = run_pass(ids, table, masses)
-    column = folded(spread, "gx")
-    even = swapped(column[: 4 * INNER], "gy", "even")
-    odd = swapped(column[8 * INNER :], "gy", "odd")
-    new_dual, site_shift = run_small(
-        finish_kernel, (dual_weight.shape, site_frac.shape), tile, masses, column, even, odd
+    summed = folded(spread, "gx")
+    even = swapped(summed[: 4 * INNER], "gy", "even")
+    odd = swapped(summed[8 * INNER :], "gy", "odd")
+    new_dual, site_shift = run_finish(
+        dual_weight, site_frac, tile, masses, summed, even, odd
     )
     return new_dual, site_shift, displacement
 

time: 64.7 us -> 63.4 us (0.980)
  waiting for transfers between devices: 18.2 us -> 16.8 us
  local copies, waits for them, and re-layouts: 2.86 us -> 1.49 us
  starting transfers between devices: 32.7 us -> 33.9 us
  other arithmetic: 0.15 us -> 0.88 us
    ppermute x16, waiting for transfers between devices: 18.2 us -> 16.8 us  [swapped(): lax.ppermute(array, axis, [(i, partner(kind, i, peers)) for i in range(pe...]
    unnamed x12 -> x6, local copies, waits for them, and re-layouts: 2.71 us -> 1.34 us
    ppermute x16, starting transfers between devices: 32.7 us -> 33.9 us  [swapped(): lax.ppermute(array, axis, [(i, partner(kind, i, peers)) for i in range(pe...]
    concatenate x0 -> x1, other arithmetic: none -> 0.71 us  [on_device(): jnp.concatenate([site_frac, dual_weight[None], target_mass[None]], 0)]
  transfers between devices with their start and end apart: 16 -> 16, of which waited for: 9 -> 8; matrix products, arithmetic and copies ran while one was open for 0% -> 0% of each run, Pallas kernels for 0% -> 0%
where the time goes in v4:
time: 63.4 us; the launch traced here: 63.2 us
  starting transfers between devices  33.9 us (53%)
  waiting for transfers between devices  16.8 us (26%)
  Pallas kernels  8.77 us (14%)
  local copies, waits for them, and re-layouts  1.49 us (2%)
  between operations  1.39 us (2%)
  other arithmetic  0.88 us (1%)
    ppermute x16, starting transfers between devices, swapped(): lax.ppermute(array, axis, [(i, partner(kind, i, peers)) for i in range(pe...  33.9 us
    ppermute x16, waiting for transfers between devices, swapped(): lax.ppermute(array, axis, [(i, partner(kind, i, peers)) for i in range(pe...  16.8 us
    pallas_call x2, Pallas kernels, run_pass(): pl.pallas_call(functools.partial(pass_kernel, moments), out_shape=shapes,...  8.17 us
    unnamed x6, local copies, waits for them, and re-layouts  1.34 us
  transfers between devices with their start and end apart: 16, of which 8 were waited for; matrix products, arithmetic and copies ran while one was open for 0% of the time, Pallas kernels for 0%

profile of v4, /device:TPU:1, one launch (start us, length us, event | category | flops | bytes accessed | tf_op | source)
XLA Modules:
  0.0 63.2 jit_solution(4918487542569472405)
XLA Ops:
  0.6 0.7 %copy-done = f32[2,2,128]{2,1,0:T(2,128)S(1)} copy-done((f32[2,2,128]{2,1,0:T(2,128)S(1)}, f32[2,2,128]{2,1,0:T(2,128)}, u32[]{:S(2)}) %copy-start) | copy-done | bytes 2072
  1.3 0.7 %pad_maximum_fusion.4.tile_ref = f32[5,2,2,128]{3,2,1,0:T(2,128)S(1)} fusion(f32[1,2,2,128]{3,2,1,0:T(2,128)S(1)} %bitcast.7, f32[1,2,2,128]{3,2,1,0:T(2,128)} %bitcast.8, f32[3,2,2,128]{3,2,1,0:T(2,128)} %param.5), kind=kLoop, calls=%fused_computation.5 | loop fusion | flops 5120 | bytes 20480 | tf_op jit(solution)/shard_map/concatenate | solution.py:274
  2.0 2.0 %collective-permute-start = (f32[5,2,2,128]{3,2,1,0:T(2,128)S(1)}, f32[5,2,2,128]{3,2,1,0:T(2,128)S(1)}, u32[]{:S(2)}, u32[]{:S(2)}) collective-permute-start(f32[5,2,2,128]{3,2,1,0:T(2,128)S(1)} %pad_maximum_fusion.4.tile_ref), channel_id=1, source_target_pairs={{0,16},{16,0},{32,48},{48,32},{64,80},{80,64},{96,112},{112,96},{1... | collective-permute-start | bytes 30728 | tf_op jit(solution)/shard_map/ppermute | solution.py:236
  4.1 7.6 %collective-permute-start.1 = (f32[5,2,2,128]{3,2,1,0:T(2,128)S(1)}, f32[5,2,2,128]{3,2,1,0:T(2,128)S(1)}, u32[]{:S(2)}, u32[]{:S(2)}) collective-permute-start(f32[5,2,2,128]{3,2,1,0:T(2,128)S(1)} %pad_maximum_fusion.4.tile_ref), channel_id=1, source_target_pairs={{0,240},{16,32},{32,16},{48,64},{64,48},{80,96},{96,80},{112,128},... | collective-permute-start | bytes 30728 | tf_op jit(solution)/shard_map/ppermute | solution.py:236
  12.3 0.0 copy-start.1
  12.3 0.6 %copy-done.1 = s32[1,1,12]{2,1,0:T(1,128)S(1)} copy-done((s32[1,1,12]{2,1,0:T(1,128)S(1)}, s32[1,1,12]{2,1,0:T(1,128)}, u32[]{:S(2)}) %copy-start.1) | copy-done | bytes 72
  12.9 0.1 pad_add_fusion.ids_ref
  13.0 0.0 collective-permute-done
  13.0 1.6 %collective-permute-start.2 = (f32[15,2,2,128]{3,2,1,0:T(2,128)S(1)}, f32[15,2,2,128]{3,2,1,0:T(2,128)S(1)}, u32[]{:S(2)}, u32[]{:S(2)}) collective-permute-start(f32[15,2,2,128]{3,2,1,0:T(2,128)S(1)} %pad_maximum_fusion), channel_id=1, source_target_pairs={{0,1},{1,0},{2,3},{3,2},{4,5},{5,4},{6,7},{7,6},{8,9},{9,8},{10,11... | collective-permute-start | bytes 92168 | tf_op jit(solution)/shard_map/ppermute | solution.py:236
  14.6 0.7 %collective-permute-start.3 = (f32[15,2,2,128]{3,2,1,0:T(2,128)S(1)}, f32[15,2,2,128]{3,2,1,0:T(2,128)S(1)}, u32[]{:S(2)}, u32[]{:S(2)}) collective-permute-start(f32[15,2,2,128]{3,2,1,0:T(2,128)S(1)} %pad_maximum_fusion), channel_id=1, source_target_pairs={{0,15},{1,2},{2,1},{3,4},{4,3},{5,6},{6,5},{7,8},{8,7},{9,10},{10,... | collective-permute-start | bytes 92168 | tf_op jit(solution)/shard_map/ppermute | solution.py:236
  15.4 0.1 collective-permute-done.2
  15.5 2.4 %collective-permute-done.3 = f32[15,2,2,128]{3,2,1,0:T(2,128)S(1)} collective-permute-done((f32[15,2,2,128]{3,2,1,0:T(2,128)S(1)}, f32[15,2,2,128]{3,2,1,0:T(2,128)S(1)}, u32[]{:S(2)}, u32[]{:S(2)}) %collective-permute-start.3) | collective-permute-done | bytes 30752 | tf_op jit(solution)/shard_map/ppermute | solution.py:236
  17.9 3.4 %shard_map.76 = f32[48,128]{1,0:T(8,128)S(1)} custom-call(s32[15]{0:T(128)S(1)} %pad_add_fusion.ids_ref, f32[45,2,2,128]{3,2,1,0:T(2,128)S(1)} %constant_dynamic-update-slice_fusion.table_ref), custom_call_target="tpu_custom_call" | custom-call | tf_op jit(solution)/shard_map/pallas_call | solution.py:190
  21.4 0.1 collective-permute-start.4
  21.5 6.0 %collective-permute-start.7 = (f32[24,128]{1,0:T(8,128)S(1)}, f32[24,128]{1,0:T(8,128)S(1)}, u32[]{:S(2)}, u32[]{:S(2)}) collective-permute-start(f32[24,128]{1,0:T(8,128)S(1)} %get-tuple-element.41), channel_id=1, source_target_pairs={{0,240},{16,32},{32,16},{48,64},{64,48},{80,96},{96,80},{112,128},... | collective-permute-start | bytes 36872 | tf_op jit(solution)/shard_map/ppermute | solution.py:236
  27.5 2.6 %collective-permute-start.6 = (f32[12,128]{1,0:T(8,128)S(1)}, f32[12,128]{1,0:T(8,128)S(1)}, u32[]{:S(2)}, u32[]{:S(2)}) collective-permute-start(f32[12,128]{1,0:T(8,128)S(1)} %get-tuple-element.24), channel_id=1, source_target_pairs={{0,224},{16,240},{32,64},{48,80},{64,32},{80,48},{96,128},{112,144... | collective-permute-start | bytes 18440 | tf_op jit(solution)/shard_map/ppermute | solution.py:236
  30.2 1.4 %collective-permute-done.5 = f32[12,128]{1,0:T(8,128)S(1)} collective-permute-done((f32[12,128]{1,0:T(8,128)S(1)}, f32[12,128]{1,0:T(8,128)S(1)}, u32[]{:S(2)}, u32[]{:S(2)}) %collective-permute-start.5) | collective-permute-done | bytes 6176 | tf_op jit(solution)/shard_map/ppermute | solution.py:236
  31.5 3.1 %collective-permute-done.6 = f32[12,128]{1,0:T(8,128)S(1)} collective-permute-done((f32[12,128]{1,0:T(8,128)S(1)}, f32[12,128]{1,0:T(8,128)S(1)}, u32[]{:S(2)}, u32[]{:S(2)}) %collective-permute-start.6) | collective-permute-done | bytes 6176 | tf_op jit(solution)/shard_map/ppermute | solution.py:236
  34.6 0.1 concatenate.48
  34.7 2.2 %collective-permute-start.11 = (f32[24,128]{1,0:T(8,128)S(1)}, f32[24,128]{1,0:T(8,128)S(1)}, u32[]{:S(2)}, u32[]{:S(2)}) collective-permute-start(f32[24,128]{1,0:T(8,128)S(1)} %concatenate.48), channel_id=1, source_target_pairs={{0,15},{1,2},{2,1},{3,4},{4,3},{5,6},{6,5},{7,8},{8,7},{9,10},{10,... | collective-permute-start | bytes 36872 | tf_op jit(solution)/shard_map/ppermute | solution.py:236
  36.9 0.1 concatenate.44
  37.0 3.5 %collective-permute-start.8 = (f32[24,128]{1,0:T(8,128)S(1)}, f32[24,128]{1,0:T(8,128)S(1)}, u32[]{:S(2)}, u32[]{:S(2)}) collective-permute-start(f32[24,128]{1,0:T(8,128)S(1)} %concatenate.44), channel_id=1, source_target_pairs={{0,1},{1,0},{2,3},{3,2},{4,5},{5,4},{6,7},{7,6},{8,9},{9,8},{10,11... | collective-permute-start | bytes 36872 | tf_op jit(solution)/shard_map/ppermute | solution.py:236
  40.5 1.5 %collective-permute-start.10 = (f32[12,128]{1,0:T(8,128)S(1)}, f32[12,128]{1,0:T(8,128)S(1)}, u32[]{:S(2)}, u32[]{:S(2)}) collective-permute-start(f32[12,128]{1,0:T(8,128)S(1)} %get-tuple-element.31), channel_id=1, source_target_pairs={{0,14},{1,15},{2,4},{3,5},{4,2},{5,3},{6,8},{7,9},{8,6},{9,7},{10,... | collective-permute-start | bytes 18440 | tf_op jit(solution)/shard_map/ppermute | solution.py:236
  42.1 0.0 collective-permute-start.9
  42.1 3.2 %collective-permute-done.10 = f32[12,128]{1,0:T(8,128)S(1)} collective-permute-done((f32[12,128]{1,0:T(8,128)S(1)}, f32[12,128]{1,0:T(8,128)S(1)}, u32[]{:S(2)}, u32[]{:S(2)}) %collective-permute-start.10) | collective-permute-done | bytes 6176 | tf_op jit(solution)/shard_map/ppermute | solution.py:236
  45.3 4.8 %shard_map.77 = (f32[144,128]{1,0:T(8,128)S(1)}, f32[3,4,4,256]{3,2,1,0:T(4,128)}) custom-call(s32[15]{0:T(128)S(1)} %pad_add_fusion.ids_ref, f32[45,2,2,128]{3,2,1,0:T(2,128)S(1)} %constant_dynamic-update-slice_fusion.table_ref, f32[36,128]{1,0:T(8,128)S(1)} %pad_maximum_fusion.1.refs_0_.masses_ref), custom_call_target="tpu_custom_call" | custom-call | tf_op jit(solution)/shard_map/pallas_call | solution.py:190
  50.1 3.4 %collective-permute-start.13 = (f32[48,128]{1,0:T(8,128)S(1)}, f32[48,128]{1,0:T(8,128)S(1)}, u32[]{:S(2)}, u32[]{:S(2)}) collective-permute-start(f32[48,128]{1,0:T(8,128)S(1)} %get-tuple-element.16), channel_id=1, source_target_pairs={{0,240},{16,32},{32,16},{48,64},{64,48},{80,96},{96,80},{112,128},... | collective-permute-start | bytes 73736 | tf_op jit(solution)/shard_map/ppermute | solution.py:236
  53.5 3.6 %collective-permute-done.13 = f32[48,128]{1,0:T(8,128)S(1)} collective-permute-done((f32[48,128]{1,0:T(8,128)S(1)}, f32[48,128]{1,0:T(8,128)S(1)}, u32[]{:S(2)}, u32[]{:S(2)}) %collective-permute-start.13) | collective-permute-done | bytes 24608 | tf_op jit(solution)/shard_map/ppermute | solution.py:236
  57.1 2.5 %collective-permute-start.14 = (f32[16,128]{1,0:T(8,128)S(1)}, f32[16,128]{1,0:T(8,128)S(1)}, u32[]{:S(2)}, u32[]{:S(2)}) collective-permute-start(f32[16,128]{1,0:T(8,128)S(1)} %get-tuple-element.21), channel_id=1, source_target_pairs={{0,1},{1,0},{2,3},{3,2},{4,5},{5,4},{6,7},{7,6},{8,9},{9,8},{10,11... | collective-permute-start | bytes 24584 | tf_op jit(solution)/shard_map/ppermute | solution.py:236
  59.6 0.8 %collective-permute-done.14.even_ref = f32[16,128]{1,0:T(8,128)S(1)} collective-permute-done((f32[16,128]{1,0:T(8,128)S(1)}, f32[16,128]{1,0:T(8,128)S(1)}, u32[]{:S(2)}, u32[]{:S(2)}) %collective-permute-start.14) | collective-permute-done | bytes 8224 | tf_op jit(solution)/shard_map/ppermute | solution.py:236
  60.4 2.2 %collective-permute-done.15.odd_ref = f32[16,128]{1,0:T(8,128)S(1)} collective-permute-done((f32[16,128]{1,0:T(8,128)S(1)}, f32[16,128]{1,0:T(8,128)S(1)}, u32[]{:S(2)}, u32[]{:S(2)}) %collective-permute-start.15) | collective-permute-done | bytes 8224 | tf_op jit(solution)/shard_map/ppermute | solution.py:236
  62.6 0.6 shard_map.78
  (26 shorter events, 0.2 us)
Async XLA Ops:
  0.6 0.7 %copy-start = (f32[2,2,128]{2,1,0:T(2,128)S(1)}, f32[2,2,128]{2,1,0:T(2,128)}, u32[]{:S(2)}) copy-start(f32[2,2,128]{2,1,0:T(2,128)} %param.7) | copy-start | bytes 6148
  2.0 11.0 %collective-permute-start = (f32[5,2,2,128]{3,2,1,0:T(2,128)S(1)}, f32[5,2,2,128]{3,2,1,0:T(2,128)S(1)}, u32[]{:S(2)}, u32[]{:S(2)}) collective-permute-start(f32[5,2,2,128]{3,2,1,0:T(2,128)S(1)} %pad_maximum_fusion.4.tile_ref), channel_id=1, source_target_pairs={{0,16},{16,0},{32,48},{48,32},{64,80},{80,64},{96,112},{112,96},{1... | collective-permute-start | bytes 30728 | tf_op jit(solution)/shard_map/ppermute | solution.py:236
  4.1 8.9 %collective-permute-start.1 = (f32[5,2,2,128]{3,2,1,0:T(2,128)S(1)}, f32[5,2,2,128]{3,2,1,0:T(2,128)S(1)}, u32[]{:S(2)}, u32[]{:S(2)}) collective-permute-start(f32[5,2,2,128]{3,2,1,0:T(2,128)S(1)} %pad_maximum_fusion.4.tile_ref), channel_id=1, source_target_pairs={{0,240},{16,32},{32,16},{48,64},{64,48},{80,96},{96,80},{112,128},... | collective-permute-start | bytes 30728 | tf_op jit(solution)/shard_map/ppermute | solution.py:236
  12.3 0.7 %copy-start.1 = (s32[1,1,12]{2,1,0:T(1,128)S(1)}, s32[1,1,12]{2,1,0:T(1,128)}, u32[]{:S(2)}) copy-start(s32[1,1,12]{2,1,0:T(1,128)} %param.8) | copy-start | bytes 148
  13.0 2.4 %collective-permute-start.2 = (f32[15,2,2,128]{3,2,1,0:T(2,128)S(1)}, f32[15,2,2,128]{3,2,1,0:T(2,128)S(1)}, u32[]{:S(2)}, u32[]{:S(2)}) collective-permute-start(f32[15,2,2,128]{3,2,1,0:T(2,128)S(1)} %pad_maximum_fusion), channel_id=1, source_target_pairs={{0,1},{1,0},{2,3},{3,2},{4,5},{5,4},{6,7},{7,6},{8,9},{9,8},{10,11... | collective-permute-start | bytes 92168 | tf_op jit(solution)/shard_map/ppermute | solution.py:236
  14.6 3.3 %collective-permute-start.3 = (f32[15,2,2,128]{3,2,1,0:T(2,128)S(1)}, f32[15,2,2,128]{3,2,1,0:T(2,128)S(1)}, u32[]{:S(2)}, u32[]{:S(2)}) collective-permute-start(f32[15,2,2,128]{3,2,1,0:T(2,128)S(1)} %pad_maximum_fusion), channel_id=1, source_target_pairs={{0,15},{1,2},{2,1},{3,4},{4,3},{5,6},{6,5},{7,8},{8,7},{9,10},{10,... | collective-permute-start | bytes 92168 | tf_op jit(solution)/shard_map/ppermute | solution.py:236
  21.4 13.2 %collective-permute-start.4 = (f32[24,128]{1,0:T(8,128)S(1)}, f32[24,128]{1,0:T(8,128)S(1)}, u32[]{:S(2)}, u32[]{:S(2)}) collective-permute-start(f32[24,128]{1,0:T(8,128)S(1)} %get-tuple-element.42), channel_id=1, source_target_pairs={{0,16},{16,0},{32,48},{48,32},{64,80},{80,64},{96,112},{112,96},{1... | collective-permute-start | bytes 36872 | tf_op jit(solution)/shard_map/ppermute | solution.py:236
  21.5 13.1 %collective-permute-start.7 = (f32[24,128]{1,0:T(8,128)S(1)}, f32[24,128]{1,0:T(8,128)S(1)}, u32[]{:S(2)}, u32[]{:S(2)}) collective-permute-start(f32[24,128]{1,0:T(8,128)S(1)} %get-tuple-element.41), channel_id=1, source_target_pairs={{0,240},{16,32},{32,16},{48,64},{64,48},{80,96},{96,80},{112,128},... | collective-permute-start | bytes 36872 | tf_op jit(solution)/shard_map/ppermute | solution.py:236
  27.5 4.0 %collective-permute-start.5 = (f32[12,128]{1,0:T(8,128)S(1)}, f32[12,128]{1,0:T(8,128)S(1)}, u32[]{:S(2)}, u32[]{:S(2)}) collective-permute-start(f32[12,128]{1,0:T(8,128)S(1)} %get-tuple-element.23), channel_id=1, source_target_pairs={{0,32},{16,48},{32,0},{48,16},{64,96},{80,112},{96,64},{112,80},{1... | collective-permute-start | bytes 18440 | tf_op jit(solution)/shard_map/ppermute | solution.py:236
  27.5 7.1 %collective-permute-start.6 = (f32[12,128]{1,0:T(8,128)S(1)}, f32[12,128]{1,0:T(8,128)S(1)}, u32[]{:S(2)}, u32[]{:S(2)}) collective-permute-start(f32[12,128]{1,0:T(8,128)S(1)} %get-tuple-element.24), channel_id=1, source_target_pairs={{0,224},{16,240},{32,64},{48,80},{64,32},{80,48},{96,128},{112,144... | collective-permute-start | bytes 18440 | tf_op jit(solution)/shard_map/ppermute | solution.py:236
  34.7 10.6 %collective-permute-start.11 = (f32[24,128]{1,0:T(8,128)S(1)}, f32[24,128]{1,0:T(8,128)S(1)}, u32[]{:S(2)}, u32[]{:S(2)}) collective-permute-start(f32[24,128]{1,0:T(8,128)S(1)} %concatenate.48), channel_id=1, source_target_pairs={{0,15},{1,2},{2,1},{3,4},{4,3},{5,6},{6,5},{7,8},{8,7},{9,10},{10,... | collective-permute-start | bytes 36872 | tf_op jit(solution)/shard_map/ppermute | solution.py:236
  37.0 8.3 %collective-permute-start.8 = (f32[24,128]{1,0:T(8,128)S(1)}, f32[24,128]{1,0:T(8,128)S(1)}, u32[]{:S(2)}, u32[]{:S(2)}) collective-permute-start(f32[24,128]{1,0:T(8,128)S(1)} %concatenate.44), channel_id=1, source_target_pairs={{0,1},{1,0},{2,3},{3,2},{4,5},{5,4},{6,7},{7,6},{8,9},{9,8},{10,11... | collective-permute-start | bytes 36872 | tf_op jit(solution)/shard_map/ppermute | solution.py:236
  40.5 4.7 %collective-permute-start.10 = (f32[12,128]{1,0:T(8,128)S(1)}, f32[12,128]{1,0:T(8,128)S(1)}, u32[]{:S(2)}, u32[]{:S(2)}) collective-permute-start(f32[12,128]{1,0:T(8,128)S(1)} %get-tuple-element.31), channel_id=1, source_target_pairs={{0,14},{1,15},{2,4},{3,5},{4,2},{5,3},{6,8},{7,9},{8,6},{9,7},{10,... | collective-permute-start | bytes 18440 | tf_op jit(solution)/shard_map/ppermute | solution.py:236
  42.1 3.2 %collective-permute-start.9 = (f32[12,128]{1,0:T(8,128)S(1)}, f32[12,128]{1,0:T(8,128)S(1)}, u32[]{:S(2)}, u32[]{:S(2)}) collective-permute-start(f32[12,128]{1,0:T(8,128)S(1)} %get-tuple-element.30), channel_id=1, source_target_pairs={{0,2},{1,3},{2,0},{3,1},{4,6},{5,7},{6,4},{7,5},{8,10},{9,11},{10,... | collective-permute-start | bytes 18440 | tf_op jit(solution)/shard_map/ppermute | solution.py:236
  50.1 3.4 %collective-permute-start.12 = (f32[48,128]{1,0:T(8,128)S(1)}, f32[48,128]{1,0:T(8,128)S(1)}, u32[]{:S(2)}, u32[]{:S(2)}) collective-permute-start(f32[48,128]{1,0:T(8,128)S(1)} %get-tuple-element.15), channel_id=1, source_target_pairs={{0,16},{16,0},{32,48},{48,32},{64,80},{80,64},{96,112},{112,96},{1... | collective-permute-start | bytes 73736 | tf_op jit(solution)/shard_map/ppermute | solution.py:236
  50.1 7.0 %collective-permute-start.13 = (f32[48,128]{1,0:T(8,128)S(1)}, f32[48,128]{1,0:T(8,128)S(1)}, u32[]{:S(2)}, u32[]{:S(2)}) collective-permute-start(f32[48,128]{1,0:T(8,128)S(1)} %get-tuple-element.16), channel_id=1, source_target_pairs={{0,240},{16,32},{32,16},{48,64},{64,48},{80,96},{96,80},{112,128},... | collective-permute-start | bytes 73736 | tf_op jit(solution)/shard_map/ppermute | solution.py:236
  57.1 3.3 %collective-permute-start.14 = (f32[16,128]{1,0:T(8,128)S(1)}, f32[16,128]{1,0:T(8,128)S(1)}, u32[]{:S(2)}, u32[]{:S(2)}) collective-permute-start(f32[16,128]{1,0:T(8,128)S(1)} %get-tuple-element.21), channel_id=1, source_target_pairs={{0,1},{1,0},{2,3},{3,2},{4,5},{5,4},{6,7},{7,6},{8,9},{9,8},{10,11... | collective-permute-start | bytes 24584 | tf_op jit(solution)/shard_map/ppermute | solution.py:236
  59.6 3.1 %collective-permute-start.15 = (f32[16,128]{1,0:T(8,128)S(1)}, f32[16,128]{1,0:T(8,128)S(1)}, u32[]{:S(2)}, u32[]{:S(2)}) collective-permute-start(f32[16,128]{1,0:T(8,128)S(1)} %get-tuple-element.20), channel_id=1, source_target_pairs={{0,15},{1,2},{2,1},{3,4},{4,3},{5,6},{6,5},{7,8},{8,7},{9,10},{10,... | collective-permute-start | bytes 24584 | tf_op jit(solution)/shard_map/ppermute | solution.py:236

commit v5 on v4

--- a/solution.py
+++ b/solution.py
@@ -99,22 +99,21 @@
         rows = pl.ds(first, CHUNK)
         at_z = lax.broadcasted_iota(jnp.int32, (CHUNK, BLOCK), 0) + first
         at_z = at_z.astype(jnp.float32) + 0.5
-        peaks = [None, None]
+        peaks, kept = [None, None], []
         for m in range(K_MAX):
             lanes = pl.ds(m * BLOCK, BLOCK)
             dz = at_z - site_ref[2:3, lanes]
             fall = dz * dz * -KAPPA
             for g in range(2):
                 t = fall + site_ref[4 + g : 5 + g, lanes]
+                kept.append(t)
                 peaks[g] = t if peaks[g] is None else jnp.maximum(peaks[g], t)
         tops = [jnp.max(p, axis=1, keepdims=True) - SHIFT for p in peaks]
         for m in range(K_MAX):
             lanes = pl.ds(m * BLOCK, BLOCK)
             dz = at_z - site_ref[2:3, lanes]
-            fall = dz * dz * -KAPPA
             for g in range(2):
-                t = fall + site_ref[4 + g : 5 + g, lanes]
-                e = jnp.exp2(t - tops[g])
+                e = jnp.exp2(kept[2 * m + g] - tops[g])
                 c_ref[2 * g, rows, lanes], c_ref[2 * g + 1, rows, lanes] = halves(e)
                 if moments:
                     d_ref[2 * g, rows, lanes], d_ref[2 * g + 1, rows, lanes] = halves(e * dz)

time: 63.4 us -> 62.9 us (level)
  no operation moved by 1% of the time
where the time goes in v5:
time: 62.9 us; the launch traced here: 62.7 us
  starting transfers between devices  33.9 us (54%)
  waiting for transfers between devices  16.8 us (27%)
  Pallas kernels  8.21 us (13%)
  local copies, waits for them, and re-layouts  1.49 us (2%)
  between operations  1.39 us (2%)
  other arithmetic  0.88 us (1%)
    ppermute x16, starting transfers between devices, swapped(): lax.ppermute(array, axis, [(i, partner(kind, i, peers)) for i in range(pe...  33.9 us
    ppermute x16, waiting for transfers between devices, swapped(): lax.ppermute(array, axis, [(i, partner(kind, i, peers)) for i in range(pe...  16.8 us
    pallas_call x2, Pallas kernels, run_pass(): pl.pallas_call(functools.partial(pass_kernel, moments), out_shape=shapes,...  7.6 us
    unnamed x6, local copies, waits for them, and re-layouts  1.34 us
  transfers between devices with their start and end apart: 16, of which 8 were waited for; matrix products, arithmetic and copies ran while one was open for 0% of the time, Pallas kernels for 0%

profile of v5, /device:TPU:1, one launch (start us, length us, event | category | flops | bytes accessed | tf_op | source)
XLA Modules:
  0.0 62.7 jit_solution(8253990883504151145)
XLA Ops:
  0.6 0.7 %copy-done = f32[2,2,128]{2,1,0:T(2,128)S(1)} copy-done((f32[2,2,128]{2,1,0:T(2,128)S(1)}, f32[2,2,128]{2,1,0:T(2,128)}, u32[]{:S(2)}) %copy-start) | copy-done | bytes 2072
  1.3 0.7 %pad_maximum_fusion.4.tile_ref = f32[5,2,2,128]{3,2,1,0:T(2,128)S(1)} fusion(f32[1,2,2,128]{3,2,1,0:T(2,128)S(1)} %bitcast.7, f32[1,2,2,128]{3,2,1,0:T(2,128)} %bitcast.8, f32[3,2,2,128]{3,2,1,0:T(2,128)} %param.5), kind=kLoop, calls=%fused_computation.5 | loop fusion | flops 5120 | bytes 20480 | tf_op jit(solution)/shard_map/concatenate | solution.py:273
  2.0 2.0 %collective-permute-start = (f32[5,2,2,128]{3,2,1,0:T(2,128)S(1)}, f32[5,2,2,128]{3,2,1,0:T(2,128)S(1)}, u32[]{:S(2)}, u32[]{:S(2)}) collective-permute-start(f32[5,2,2,128]{3,2,1,0:T(2,128)S(1)} %pad_maximum_fusion.4.tile_ref), channel_id=1, source_target_pairs={{0,16},{16,0},{32,48},{48,32},{64,80},{80,64},{96,112},{112,96},{1... | collective-permute-start | bytes 30728 | tf_op jit(solution)/shard_map/ppermute | solution.py:235
  4.1 7.6 %collective-permute-start.1 = (f32[5,2,2,128]{3,2,1,0:T(2,128)S(1)}, f32[5,2,2,128]{3,2,1,0:T(2,128)S(1)}, u32[]{:S(2)}, u32[]{:S(2)}) collective-permute-start(f32[5,2,2,128]{3,2,1,0:T(2,128)S(1)} %pad_maximum_fusion.4.tile_ref), channel_id=1, source_target_pairs={{0,240},{16,32},{32,16},{48,64},{64,48},{80,96},{96,80},{112,128},... | collective-permute-start | bytes 30728 | tf_op jit(solution)/shard_map/ppermute | solution.py:235
  12.3 0.0 copy-start.1
  12.3 0.6 %copy-done.1 = s32[1,1,12]{2,1,0:T(1,128)S(1)} copy-done((s32[1,1,12]{2,1,0:T(1,128)S(1)}, s32[1,1,12]{2,1,0:T(1,128)}, u32[]{:S(2)}) %copy-start.1) | copy-done | bytes 72
  12.9 0.1 pad_add_fusion.ids_ref
  13.0 0.0 collective-permute-done
  13.0 1.6 %collective-permute-start.2 = (f32[15,2,2,128]{3,2,1,0:T(2,128)S(1)}, f32[15,2,2,128]{3,2,1,0:T(2,128)S(1)}, u32[]{:S(2)}, u32[]{:S(2)}) collective-permute-start(f32[15,2,2,128]{3,2,1,0:T(2,128)S(1)} %pad_maximum_fusion), channel_id=1, source_target_pairs={{0,1},{1,0},{2,3},{3,2},{4,5},{5,4},{6,7},{7,6},{8,9},{9,8},{10,11... | collective-permute-start | bytes 92168 | tf_op jit(solution)/shard_map/ppermute | solution.py:235
  14.6 0.7 %collective-permute-start.3 = (f32[15,2,2,128]{3,2,1,0:T(2,128)S(1)}, f32[15,2,2,128]{3,2,1,0:T(2,128)S(1)}, u32[]{:S(2)}, u32[]{:S(2)}) collective-permute-start(f32[15,2,2,128]{3,2,1,0:T(2,128)S(1)} %pad_maximum_fusion), channel_id=1, source_target_pairs={{0,15},{1,2},{2,1},{3,4},{4,3},{5,6},{6,5},{7,8},{8,7},{9,10},{10,... | collective-permute-start | bytes 92168 | tf_op jit(solution)/shard_map/ppermute | solution.py:235
  15.4 0.1 collective-permute-done.2
  15.5 2.4 %collective-permute-done.3 = f32[15,2,2,128]{3,2,1,0:T(2,128)S(1)} collective-permute-done((f32[15,2,2,128]{3,2,1,0:T(2,128)S(1)}, f32[15,2,2,128]{3,2,1,0:T(2,128)S(1)}, u32[]{:S(2)}, u32[]{:S(2)}) %collective-permute-start.3) | collective-permute-done | bytes 30752 | tf_op jit(solution)/shard_map/ppermute | solution.py:235
  17.9 3.0 %shard_map.76 = f32[48,128]{1,0:T(8,128)S(1)} custom-call(s32[15]{0:T(128)S(1)} %pad_add_fusion.ids_ref, f32[45,2,2,128]{3,2,1,0:T(2,128)S(1)} %constant_dynamic-update-slice_fusion.table_ref), custom_call_target="tpu_custom_call" | custom-call | tf_op jit(solution)/shard_map/pallas_call | solution.py:189
  21.0 0.1 collective-permute-start.4
  21.1 6.0 %collective-permute-start.7 = (f32[24,128]{1,0:T(8,128)S(1)}, f32[24,128]{1,0:T(8,128)S(1)}, u32[]{:S(2)}, u32[]{:S(2)}) collective-permute-start(f32[24,128]{1,0:T(8,128)S(1)} %get-tuple-element.41), channel_id=1, source_target_pairs={{0,240},{16,32},{32,16},{48,64},{64,48},{80,96},{96,80},{112,128},... | collective-permute-start | bytes 36872 | tf_op jit(solution)/shard_map/ppermute | solution.py:235
  27.1 2.6 %collective-permute-start.6 = (f32[12,128]{1,0:T(8,128)S(1)}, f32[12,128]{1,0:T(8,128)S(1)}, u32[]{:S(2)}, u32[]{:S(2)}) collective-permute-start(f32[12,128]{1,0:T(8,128)S(1)} %get-tuple-element.24), channel_id=1, source_target_pairs={{0,224},{16,240},{32,64},{48,80},{64,32},{80,48},{96,128},{112,144... | collective-permute-start | bytes 18440 | tf_op jit(solution)/shard_map/ppermute | solution.py:235
  29.8 1.4 %collective-permute-done.5 = f32[12,128]{1,0:T(8,128)S(1)} collective-permute-done((f32[12,128]{1,0:T(8,128)S(1)}, f32[12,128]{1,0:T(8,128)S(1)}, u32[]{:S(2)}, u32[]{:S(2)}) %collective-permute-start.5) | collective-permute-done | bytes 6176 | tf_op jit(solution)/shard_map/ppermute | solution.py:235
  31.1 3.0 %collective-permute-done.6 = f32[12,128]{1,0:T(8,128)S(1)} collective-permute-done((f32[12,128]{1,0:T(8,128)S(1)}, f32[12,128]{1,0:T(8,128)S(1)}, u32[]{:S(2)}, u32[]{:S(2)}) %collective-permute-start.6) | collective-permute-done | bytes 6176 | tf_op jit(solution)/shard_map/ppermute | solution.py:235
  34.2 0.1 concatenate.48
  34.3 2.2 %collective-permute-start.11 = (f32[24,128]{1,0:T(8,128)S(1)}, f32[24,128]{1,0:T(8,128)S(1)}, u32[]{:S(2)}, u32[]{:S(2)}) collective-permute-start(f32[24,128]{1,0:T(8,128)S(1)} %concatenate.48), channel_id=1, source_target_pairs={{0,15},{1,2},{2,1},{3,4},{4,3},{5,6},{6,5},{7,8},{8,7},{9,10},{10,... | collective-permute-start | bytes 36872 | tf_op jit(solution)/shard_map/ppermute | solution.py:235
  36.5 0.1 concatenate.44
  36.6 3.5 %collective-permute-start.8 = (f32[24,128]{1,0:T(8,128)S(1)}, f32[24,128]{1,0:T(8,128)S(1)}, u32[]{:S(2)}, u32[]{:S(2)}) collective-permute-start(f32[24,128]{1,0:T(8,128)S(1)} %concatenate.44), channel_id=1, source_target_pairs={{0,1},{1,0},{2,3},{3,2},{4,5},{5,4},{6,7},{7,6},{8,9},{9,8},{10,11... | collective-permute-start | bytes 36872 | tf_op jit(solution)/shard_map/ppermute | solution.py:235
  40.2 1.5 %collective-permute-start.10 = (f32[12,128]{1,0:T(8,128)S(1)}, f32[12,128]{1,0:T(8,128)S(1)}, u32[]{:S(2)}, u32[]{:S(2)}) collective-permute-start(f32[12,128]{1,0:T(8,128)S(1)} %get-tuple-element.31), channel_id=1, source_target_pairs={{0,14},{1,15},{2,4},{3,5},{4,2},{5,3},{6,8},{7,9},{8,6},{9,7},{10,... | collective-permute-start | bytes 18440 | tf_op jit(solution)/shard_map/ppermute | solution.py:235
  41.7 0.0 collective-permute-start.9
  41.7 3.2 %collective-permute-done.10 = f32[12,128]{1,0:T(8,128)S(1)} collective-permute-done((f32[12,128]{1,0:T(8,128)S(1)}, f32[12,128]{1,0:T(8,128)S(1)}, u32[]{:S(2)}, u32[]{:S(2)}) %collective-permute-start.10) | collective-permute-done | bytes 6176 | tf_op jit(solution)/shard_map/ppermute | solution.py:235
  44.9 4.6 %shard_map.77 = (f32[144,128]{1,0:T(8,128)S(1)}, f32[3,4,4,256]{3,2,1,0:T(4,128)}) custom-call(s32[15]{0:T(128)S(1)} %pad_add_fusion.ids_ref, f32[45,2,2,128]{3,2,1,0:T(2,128)S(1)} %constant_dynamic-update-slice_fusion.table_ref, f32[36,128]{1,0:T(8,128)S(1)} %pad_maximum_fusion.1.refs_0_.masses_ref), custom_call_target="tpu_custom_call" | custom-call | tf_op jit(solution)/shard_map/pallas_call | solution.py:189
  49.5 3.4 %collective-permute-start.13 = (f32[48,128]{1,0:T(8,128)S(1)}, f32[48,128]{1,0:T(8,128)S(1)}, u32[]{:S(2)}, u32[]{:S(2)}) collective-permute-start(f32[48,128]{1,0:T(8,128)S(1)} %get-tuple-element.16), channel_id=1, source_target_pairs={{0,240},{16,32},{32,16},{48,64},{64,48},{80,96},{96,80},{112,128},... | collective-permute-start | bytes 73736 | tf_op jit(solution)/shard_map/ppermute | solution.py:235
  52.9 3.6 %collective-permute-done.13 = f32[48,128]{1,0:T(8,128)S(1)} collective-permute-done((f32[48,128]{1,0:T(8,128)S(1)}, f32[48,128]{1,0:T(8,128)S(1)}, u32[]{:S(2)}, u32[]{:S(2)}) %collective-permute-start.13) | collective-permute-done | bytes 24608 | tf_op jit(solution)/shard_map/ppermute | solution.py:235
  56.5 2.5 %collective-permute-start.14 = (f32[16,128]{1,0:T(8,128)S(1)}, f32[16,128]{1,0:T(8,128)S(1)}, u32[]{:S(2)}, u32[]{:S(2)}) collective-permute-start(f32[16,128]{1,0:T(8,128)S(1)} %get-tuple-element.21), channel_id=1, source_target_pairs={{0,1},{1,0},{2,3},{3,2},{4,5},{5,4},{6,7},{7,6},{8,9},{9,8},{10,11... | collective-permute-start | bytes 24584 | tf_op jit(solution)/shard_map/ppermute | solution.py:235
  59.0 0.8 %collective-permute-done.14.even_ref = f32[16,128]{1,0:T(8,128)S(1)} collective-permute-done((f32[16,128]{1,0:T(8,128)S(1)}, f32[16,128]{1,0:T(8,128)S(1)}, u32[]{:S(2)}, u32[]{:S(2)}) %collective-permute-start.14) | collective-permute-done | bytes 8224 | tf_op jit(solution)/shard_map/ppermute | solution.py:235
  59.8 2.2 %collective-permute-done.15.odd_ref = f32[16,128]{1,0:T(8,128)S(1)} collective-permute-done((f32[16,128]{1,0:T(8,128)S(1)}, f32[16,128]{1,0:T(8,128)S(1)}, u32[]{:S(2)}, u32[]{:S(2)}) %collective-permute-start.15) | collective-permute-done | bytes 8224 | tf_op jit(solution)/shard_map/ppermute | solution.py:235
  62.1 0.6 shard_map.78
  (26 shorter events, 0.2 us)
Async XLA Ops:
  0.6 0.7 %copy-start = (f32[2,2,128]{2,1,0:T(2,128)S(1)}, f32[2,2,128]{2,1,0:T(2,128)}, u32[]{:S(2)}) copy-start(f32[2,2,128]{2,1,0:T(2,128)} %param.7) | copy-start | bytes 6148
  2.0 11.0 %collective-permute-start = (f32[5,2,2,128]{3,2,1,0:T(2,128)S(1)}, f32[5,2,2,128]{3,2,1,0:T(2,128)S(1)}, u32[]{:S(2)}, u32[]{:S(2)}) collective-permute-start(f32[5,2,2,128]{3,2,1,0:T(2,128)S(1)} %pad_maximum_fusion.4.tile_ref), channel_id=1, source_target_pairs={{0,16},{16,0},{32,48},{48,32},{64,80},{80,64},{96,112},{112,96},{1... | collective-permute-start | bytes 30728 | tf_op jit(solution)/shard_map/ppermute | solution.py:235
  4.1 8.9 %collective-permute-start.1 = (f32[5,2,2,128]{3,2,1,0:T(2,128)S(1)}, f32[5,2,2,128]{3,2,1,0:T(2,128)S(1)}, u32[]{:S(2)}, u32[]{:S(2)}) collective-permute-start(f32[5,2,2,128]{3,2,1,0:T(2,128)S(1)} %pad_maximum_fusion.4.tile_ref), channel_id=1, source_target_pairs={{0,240},{16,32},{32,16},{48,64},{64,48},{80,96},{96,80},{112,128},... | collective-permute-start | bytes 30728 | tf_op jit(solution)/shard_map/ppermute | solution.py:235
  12.3 0.7 %copy-start.1 = (s32[1,1,12]{2,1,0:T(1,128)S(1)}, s32[1,1,12]{2,1,0:T(1,128)}, u32[]{:S(2)}) copy-start(s32[1,1,12]{2,1,0:T(1,128)} %param.8) | copy-start | bytes 148
  13.0 2.4 %collective-permute-start.2 = (f32[15,2,2,128]{3,2,1,0:T(2,128)S(1)}, f32[15,2,2,128]{3,2,1,0:T(2,128)S(1)}, u32[]{:S(2)}, u32[]{:S(2)}) collective-permute-start(f32[15,2,2,128]{3,2,1,0:T(2,128)S(1)} %pad_maximum_fusion), channel_id=1, source_target_pairs={{0,1},{1,0},{2,3},{3,2},{4,5},{5,4},{6,7},{7,6},{8,9},{9,8},{10,11... | collective-permute-start | bytes 92168 | tf_op jit(solution)/shard_map/ppermute | solution.py:235
  14.6 3.3 %collective-permute-start.3 = (f32[15,2,2,128]{3,2,1,0:T(2,128)S(1)}, f32[15,2,2,128]{3,2,1,0:T(2,128)S(1)}, u32[]{:S(2)}, u32[]{:S(2)}) collective-permute-start(f32[15,2,2,128]{3,2,1,0:T(2,128)S(1)} %pad_maximum_fusion), channel_id=1, source_target_pairs={{0,15},{1,2},{2,1},{3,4},{4,3},{5,6},{6,5},{7,8},{8,7},{9,10},{10,... | collective-permute-start | bytes 92168 | tf_op jit(solution)/shard_map/ppermute | solution.py:235
  21.0 13.2 %collective-permute-start.4 = (f32[24,128]{1,0:T(8,128)S(1)}, f32[24,128]{1,0:T(8,128)S(1)}, u32[]{:S(2)}, u32[]{:S(2)}) collective-permute-start(f32[24,128]{1,0:T(8,128)S(1)} %get-tuple-element.42), channel_id=1, source_target_pairs={{0,16},{16,0},{32,48},{48,32},{64,80},{80,64},{96,112},{112,96},{1... | collective-permute-start | bytes 36872 | tf_op jit(solution)/shard_map/ppermute | solution.py:235
  21.1 13.1 %collective-permute-start.7 = (f32[24,128]{1,0:T(8,128)S(1)}, f32[24,128]{1,0:T(8,128)S(1)}, u32[]{:S(2)}, u32[]{:S(2)}) collective-permute-start(f32[24,128]{1,0:T(8,128)S(1)} %get-tuple-element.41), channel_id=1, source_target_pairs={{0,240},{16,32},{32,16},{48,64},{64,48},{80,96},{96,80},{112,128},... | collective-permute-start | bytes 36872 | tf_op jit(solution)/shard_map/ppermute | solution.py:235
  27.1 4.0 %collective-permute-start.5 = (f32[12,128]{1,0:T(8,128)S(1)}, f32[12,128]{1,0:T(8,128)S(1)}, u32[]{:S(2)}, u32[]{:S(2)}) collective-permute-start(f32[12,128]{1,0:T(8,128)S(1)} %get-tuple-element.23), channel_id=1, source_target_pairs={{0,32},{16,48},{32,0},{48,16},{64,96},{80,112},{96,64},{112,80},{1... | collective-permute-start | bytes 18440 | tf_op jit(solution)/shard_map/ppermute | solution.py:235
  27.1 7.1 %collective-permute-start.6 = (f32[12,128]{1,0:T(8,128)S(1)}, f32[12,128]{1,0:T(8,128)S(1)}, u32[]{:S(2)}, u32[]{:S(2)}) collective-permute-start(f32[12,128]{1,0:T(8,128)S(1)} %get-tuple-element.24), channel_id=1, source_target_pairs={{0,224},{16,240},{32,64},{48,80},{64,32},{80,48},{96,128},{112,144... | collective-permute-start | bytes 18440 | tf_op jit(solution)/shard_map/ppermute | solution.py:235
  34.3 10.6 %collective-permute-start.11 = (f32[24,128]{1,0:T(8,128)S(1)}, f32[24,128]{1,0:T(8,128)S(1)}, u32[]{:S(2)}, u32[]{:S(2)}) collective-permute-start(f32[24,128]{1,0:T(8,128)S(1)} %concatenate.48), channel_id=1, source_target_pairs={{0,15},{1,2},{2,1},{3,4},{4,3},{5,6},{6,5},{7,8},{8,7},{9,10},{10,... | collective-permute-start | bytes 36872 | tf_op jit(solution)/shard_map/ppermute | solution.py:235
  36.6 8.3 %collective-permute-start.8 = (f32[24,128]{1,0:T(8,128)S(1)}, f32[24,128]{1,0:T(8,128)S(1)}, u32[]{:S(2)}, u32[]{:S(2)}) collective-permute-start(f32[24,128]{1,0:T(8,128)S(1)} %concatenate.44), channel_id=1, source_target_pairs={{0,1},{1,0},{2,3},{3,2},{4,5},{5,4},{6,7},{7,6},{8,9},{9,8},{10,11... | collective-permute-start | bytes 36872 | tf_op jit(solution)/shard_map/ppermute | solution.py:235
  40.2 4.7 %collective-permute-start.10 = (f32[12,128]{1,0:T(8,128)S(1)}, f32[12,128]{1,0:T(8,128)S(1)}, u32[]{:S(2)}, u32[]{:S(2)}) collective-permute-start(f32[12,128]{1,0:T(8,128)S(1)} %get-tuple-element.31), channel_id=1, source_target_pairs={{0,14},{1,15},{2,4},{3,5},{4,2},{5,3},{6,8},{7,9},{8,6},{9,7},{10,... | collective-permute-start | bytes 18440 | tf_op jit(solution)/shard_map/ppermute | solution.py:235
  41.7 3.2 %collective-permute-start.9 = (f32[12,128]{1,0:T(8,128)S(1)}, f32[12,128]{1,0:T(8,128)S(1)}, u32[]{:S(2)}, u32[]{:S(2)}) collective-permute-start(f32[12,128]{1,0:T(8,128)S(1)} %get-tuple-element.30), channel_id=1, source_target_pairs={{0,2},{1,3},{2,0},{3,1},{4,6},{5,7},{6,4},{7,5},{8,10},{9,11},{10,... | collective-permute-start | bytes 18440 | tf_op jit(solution)/shard_map/ppermute | solution.py:235
  49.5 3.4 %collective-permute-start.12 = (f32[48,128]{1,0:T(8,128)S(1)}, f32[48,128]{1,0:T(8,128)S(1)}, u32[]{:S(2)}, u32[]{:S(2)}) collective-permute-start(f32[48,128]{1,0:T(8,128)S(1)} %get-tuple-element.15), channel_id=1, source_target_pairs={{0,16},{16,0},{32,48},{48,32},{64,80},{80,64},{96,112},{112,96},{1... | collective-permute-start | bytes 73736 | tf_op jit(solution)/shard_map/ppermute | solution.py:235
  49.5 7.0 %collective-permute-start.13 = (f32[48,128]{1,0:T(8,128)S(1)}, f32[48,128]{1,0:T(8,128)S(1)}, u32[]{:S(2)}, u32[]{:S(2)}) collective-permute-start(f32[48,128]{1,0:T(8,128)S(1)} %get-tuple-element.16), channel_id=1, source_target_pairs={{0,240},{16,32},{32,16},{48,64},{64,48},{80,96},{96,80},{112,128},... | collective-permute-start | bytes 73736 | tf_op jit(solution)/shard_map/ppermute | solution.py:235
  56.5 3.3 %collective-permute-start.14 = (f32[16,128]{1,0:T(8,128)S(1)}, f32[16,128]{1,0:T(8,128)S(1)}, u32[]{:S(2)}, u32[]{:S(2)}) collective-permute-start(f32[16,128]{1,0:T(8,128)S(1)} %get-tuple-element.21), channel_id=1, source_target_pairs={{0,1},{1,0},{2,3},{3,2},{4,5},{5,4},{6,7},{7,6},{8,9},{9,8},{10,11... | collective-permute-start | bytes 24584 | tf_op jit(solution)/shard_map/ppermute | solution.py:235
  59.0 3.1 %collective-permute-start.15 = (f32[16,128]{1,0:T(8,128)S(1)}, f32[16,128]{1,0:T(8,128)S(1)}, u32[]{:S(2)}, u32[]{:S(2)}) collective-permute-start(f32[16,128]{1,0:T(8,128)S(1)} %get-tuple-element.20), channel_id=1, source_target_pairs={{0,15},{1,2},{2,1},{3,4},{4,3},{5,6},{6,5},{7,8},{8,7},{9,10},{10,... | collective-permute-start | bytes 24584 | tf_op jit(solution)/shard_map/ppermute | solution.py:235
